TPU v7x, 512 devices: a whole 4x4x16 slice. The times are simulated.
512 devices in a mesh: clu: 128 (over z, y, core), head: 4 (over x).
Axes of the slice: x: 4, y: 4, z: 16, core: 2. Of those that a mesh axis runs over, the one named last changes fastest.
Arguments:
- query: bfloat16 [40960, 3072], P('clu', 'head'), may hold values from -200 to 200
- key: bfloat16 [40960, 3072], P('clu', 'head'), may hold values from -6.1 to 6.1
- value: bfloat16 [40960, 3072], P('clu', 'head'), may hold values from -6 to 6
- labels: int32 [40960], P('clu'), may hold values from 0 to 2559, as said below
- partners: int32 [2560, 3], replicated, may hold values from 0 to 2559, as said below
- out_weight: bfloat16 [3072, 3072], P('head', 'clu'), may hold values from -0.109375 to 0.109375
Outputs:
- mixed: bfloat16 [40960, 3072], P('clu', 'head')
Inputs may be any that keep to these rules, and one draw needn't show every extreme that they name: Every cluster has exactly 16 tokens. Among the 320 tokens of one aligned block, at most 4 have labels in any one group of 20 consecutive clusters (same labels // 20), and some group reaches 4 in every block. For the 20 clusters of one group (same g // 20), all their listed partners are distinct and lie outside that group, and at most 1 of them lie in any one other group, a bound that some other group reaches for every group.
All inputs are finite; a program needn't handle non-finite values.
Results may differ from a plain program's by a relative error of at most 0.013.
Values may be sent and summed in bfloat16 or wider, within the bound.
A program may use at most 128 MiB of HBM per device.

v0:
```python
import math

import jax
import jax.numpy as jnp
from jax import lax
from jax.sharding import PartitionSpec as P

HD = 128
CSIZE = 16


def rank_within(owner_ids, count):
    hits = (owner_ids[..., None] == jnp.arange(count, dtype=jnp.int32)).astype(jnp.int32)
    return jnp.sum(jnp.cumsum(hits, axis=-2) * hits, axis=-1) - 1


def shards(query, key, value, labels, partners, out_weight):
    groups = lax.axis_size("clu")
    device = lax.axis_index("clu")
    tokens_here = query.shape[0]
    features = query.shape[1]
    per_device = tokens_here // CSIZE
    listed = partners.shape[1]
    token_slots = (3 * tokens_here + 2 * groups - 1) // (2 * groups)
    block_slots = max(
        (2 * per_device * listed + groups - 1) // groups,
        (per_device * listed + groups - 2) // (groups - 1),
    )
    owner = labels // per_device
    slot = owner * token_slots + rank_within(owner, groups)
    tags = jnp.full((groups * token_slots,), -1, jnp.int32).at[slot].set(labels)
    rows = jnp.stack([query, key, value], axis=1)
    arrived = lax.all_to_all(
        jnp.zeros((groups * token_slots,) + rows.shape[1:], rows.dtype).at[slot].set(rows),
        "clu",
        split_axis=0,
        concat_axis=0,
        tiled=True,
    )
    arrival_tags = lax.all_to_all(tags, "clu", split_axis=0, concat_axis=0, tiled=True)
    kv_arrived = arrived[:, 1:]
    valid = arrival_tags >= 0
    local_safe = jnp.where(valid, arrival_tags - device * per_device, per_device)
    position = rank_within(local_safe, per_device)
    destination = jnp.where(valid, local_safe * CSIZE + position, tokens_here)
    source_slot = (
        jnp.zeros((tokens_here,), jnp.int32)
        .at[destination]
        .set(jnp.arange(groups * token_slots, dtype=jnp.int32), mode="drop")
    )
    kv_here = kv_arrived[source_slot]
    wanted = partners.reshape(groups, per_device * listed)
    from_me = wanted // per_device == device
    sequence = jnp.cumsum(from_me.astype(jnp.int32), axis=1) - 1
    target = jnp.where(
        from_me,
        jnp.arange(groups, dtype=jnp.int32)[:, None] * block_slots + sequence,
        groups * block_slots,
    )
    pick = (
        jnp.zeros((groups * block_slots,), jnp.int32)
        .at[target.reshape(-1)]
        .set((wanted - device * per_device).reshape(-1), mode="drop")
    )
    cluster_blocks = kv_here.reshape(per_device, CSIZE, 2, features)
    fetched = lax.all_to_all(cluster_blocks[pick], "clu", split_axis=0, concat_axis=0, tiled=True)
    my_list = lax.dynamic_slice_in_dim(wanted, device, 1, 0)[0]
    source_owner = my_list // per_device
    location = source_owner * block_slots + rank_within(source_owner, groups)
    listed_blocks = fetched[location].reshape(per_device, listed * CSIZE, 2, features)
    queries_here = arrived[source_slot, 0]
    heads_here = features // HD
    query_blocks = queries_here.reshape(per_device, CSIZE, heads_here, HD)
    all_keys = jnp.concatenate([cluster_blocks[:, :, 0], listed_blocks[:, :, 0]], axis=1).reshape(
        per_device, (1 + listed) * CSIZE, heads_here, HD
    )
    all_values = jnp.concatenate([cluster_blocks[:, :, 1], listed_blocks[:, :, 1]], axis=1).reshape(
        per_device, (1 + listed) * CSIZE, heads_here, HD
    )
    scores = jnp.einsum(
        "cqhd,ckhd->chqk", query_blocks, all_keys, preferred_element_type=jnp.float32
    ) * (1.0 / math.sqrt(HD))
    highest = jnp.max(scores, axis=-1, keepdims=True)
    powers = jnp.exp(scores - highest)
    weights = (powers / jnp.sum(powers, axis=-1, keepdims=True)).astype(jnp.bfloat16)
    attended = jnp.einsum(
        "chqk,ckhd->cqhd", weights, all_values, preferred_element_type=jnp.float32
    ).astype(jnp.bfloat16)
    attended = attended.reshape(tokens_here, features)
    padded = jnp.concatenate([attended, jnp.zeros((1, features), jnp.bfloat16)], axis=0)
    returned = lax.all_to_all(padded[destination], "clu", split_axis=0, concat_axis=0, tiled=True)
    token_rows = returned[slot]
    partial_value = jnp.dot(
        token_rows,
        lax.all_gather(out_weight, "clu", axis=1, tiled=True),
        preferred_element_type=jnp.float32,
    )
    return lax.psum_scatter(
        partial_value.astype(jnp.bfloat16), "head", scatter_dimension=1, tiled=True
    )


def solution(mesh):
    return jax.shard_map(
        shards,
        mesh=mesh,
        in_specs=(
            P("clu", "head"),
            P("clu", "head"),
            P("clu", "head"),
            P("clu"),
            P(),
            P("head", "clu"),
        ),
        out_specs=P("clu", "head"),
        check_vma=False,
    )
```

profile of v0, /device:TPU:1, one launch (start us, length us, event | category | flops | bytes accessed | tf_op | source)
XLA Modules:
  0.0 667.2 jit_solution(11736879752408459426)
XLA Ops:
  6.5 0.8 add_select_fusion.2
  8.7 3.1 scatter_custom_fusion.1
  11.8 0.7 all_to_all.21
  12.5 20.6 %all-to-all-start.1 = ((s32[128,4,1]{1,2,0:T(1,128)}), s32[128,4,1]{1,2,0:T(1,128)S(1)}, u32[]{:S(2)}, u32[]{:S(2)}) async-start(s32[128,4,1]{1,2,0:T(1,128)} %bitcast.7), calls=%async_computation.1 | async-start | bytes 131072 | tf_op jit(solution)/shard_map/all_to_all | solution.py:40
  33.3 1.3 copy.76
  34.5 2.5 broadcast_in_dim.23
  37.0 37.5 %scatter_fusion = bf16[512,3,768]{2,1,0:T(4,128)(2,1)} fusion(bf16[512,3,768]{2,1,0:T(4,128)(2,1)} %broadcast_in_dim.23, s32[320]{0:T(512)S(1)} %compare_select_fusion.6, bf16[320,3,768]{2,1,0:T(4,128)(2,1)S(1)} %copy.76), kind=kCustom, calls=%fused_computation.6 | custom fusion | bytes 4424960 | tf_op jit(solution)/shard_map/scatter | solution.py:34
  74.5 16.6 %all-to-all-start = ((bf16[512,3,768]{2,1,0:T(4,128)(2,1)}), bf16[512,3,768]{2,1,0:T(4,128)(2,1)S(1)}, u32[]{:S(2)}, u32[]{:S(2)}) async-start(bf16[512,3,768]{2,1,0:T(4,128)(2,1)} %scatter_fusion), calls=%async_computation | async-start | bytes 6291456 | tf_op jit(solution)/shard_map/all_to_all | solution.py:33
  91.2 1.5 copy.82
  92.7 1.7 reshape.342
  94.7 0.7 add.179
  96.1 1.5 copy.81
  97.6 2.8 div.57
  101.1 1.7 and.44
  102.7 2.3 copy.87
  105.0 2.2 reshape.421
  107.4 28.6 %scatter_custom_fusion.3 = s32[128]{0:T(128)S(1)} fusion(s32[7680]{0:T(1024)S(1)} %fusion.36, s32[7680]{0:T(1024)S(1)} %reshape.421, s32[]{:T(128)} %constant.31.clone.1), kind=kCustom, calls=%fused_computation.100 | custom fusion | bytes 516 | tf_op jit(solution)/shard_map/scatter | solution.py:63
  136.5 0.9 fusion.56
  137.5 1.2 reduce-window.16
  139.7 3.0 scatter_custom_fusion.2
  142.7 88.9 %all-to-all-done = bf16[512,3,768]{2,1,0:T(4,128)(2,1)S(1)} async-done(((bf16[512,3,768]{2,1,0:T(4,128)(2,1)}), bf16[512,3,768]{2,1,0:T(4,128)(2,1)S(1)}, u32[]{:S(2)}, u32[]{:S(2)}) %all-to-all-start) | async-done | bytes 2359328 | tf_op jit(solution)/shard_map/all_to_all | solution.py:33
  231.6 2.8 slice.55
  234.4 5.1 gather_fusion
  239.5 1.3 copy.88
  240.9 3.6 gather_fusion.1
  244.5 12.1 %all-to-all-start.2 = ((bf16[128,16,2,768]{3,1,2,0:T(8,128)(2,1)}), bf16[128,16,2,768]{3,1,2,0:T(8,128)(2,1)}, u32[]{:S(2)}, u32[]{:S(2)}) async-start(bf16[128,16,2,768]{3,1,2,0:T(8,128)(2,1)} %gather_fusion.1), calls=%async_computation.2 | async-start | bytes 12582912 | tf_op jit(solution)/shard_map/all_to_all | solution.py:66
  259.1 1.7 copy.92
  260.8 12.8 %gather_fusion.3 = bf16[320,768]{1,0:T(8,128)(2,1)S(1)} fusion(bf16[512,3,768]{2,0,1:T(8,128)(2,1)} %copy.92, s32[320]{0:T(512)S(1)} %get-tuple-element.18), kind=kCustom, calls=%fused_computation.3 | custom fusion | bytes 985600 | tf_op jit(solution)/shard_map/gather | solution.py:71
  273.6 1.4 reshape.344
  275.0 4.0 slice_reduce_fusion.1
  279.1 0.9 copy_bitcast_fusion.2
  280.0 0.9 copy_bitcast_fusion.1
  280.8 264.9 %all-to-all-done.2 = bf16[128,16,2,768]{3,1,2,0:T(8,128)(2,1)} async-done(((bf16[128,16,2,768]{3,1,2,0:T(8,128)(2,1)}), bf16[128,16,2,768]{3,1,2,0:T(8,128)(2,1)}, u32[]{:S(2)}, u32[]{:S(2)}) %all-to-all-start.2) | async-done | bytes 6291488 | tf_op jit(solution)/shard_map/all_to_all | solution.py:66
  545.7 3.5 gather_fusion.2
  549.5 1.3 fusion.57
  550.8 3.3 concatenate.27
  554.1 1.3 copy.95
  555.4 1.7 concatenate.23
  557.1 1.3 copy.91
  559.0 3.6 fusion.58
  562.6 1.9 fusion.17
  564.8 2.0 gather_fusion.4
  566.8 1.1 all_to_all.24
  567.9 12.5 %all-to-all-start.3 = ((bf16[128,4,768]{2,1,0:T(4,128)(2,1)}), bf16[128,4,768]{2,1,0:T(4,128)(2,1)S(1)}, u32[]{:S(2)}, u32[]{:S(2)}) async-start(bf16[128,4,768]{2,1,0:T(4,128)(2,1)} %all_to_all.24), calls=%async_computation.3 | async-start | bytes 1572864 | tf_op jit(solution)/shard_map/all_to_all | solution.py:91
  580.4 41.3 %all-to-all-done.3 = bf16[128,4,768]{2,1,0:T(4,128)(2,1)S(1)} async-done(((bf16[128,4,768]{2,1,0:T(4,128)(2,1)}), bf16[128,4,768]{2,1,0:T(4,128)(2,1)S(1)}, u32[]{:S(2)}, u32[]{:S(2)}) %all-to-all-start.3) | async-done | bytes 786464 | tf_op jit(solution)/shard_map/all_to_all | solution.py:91
  621.9 2.1 gather_fusion.5
  624.1 5.3 convolution_convert_fusion
  629.4 30.7 %reduce-scatter.2.cloned.1.call-done = bf16[320,768]{1,0:T(8,128)(2,1)} async-done(((bf16[320,3072]{1,0:T(8,128)(2,1)}), bf16[320,768]{1,0:T(8,128)(2,1)}) %reduce-scatter.2.cloned.1.call-update) | async-done | bytes 491536 | tf_op jit(solution)/shard_map/reduce_scatter | solution.py:98
  (89 shorter events, 8.6 us)
Async XLA Ops:
  6.5 26.5 %copy-start.7 = (bf16[320,768]{1,0:T(8,128)(2,1)S(1)}, bf16[320,768]{1,0:T(8,128)(2,1)}, u32[]{:S(2)}) copy-start(bf16[320,768]{1,0:T(8,128)(2,1)} %param.6) | copy-start | bytes 1474564
  6.5 26.5 %copy-start.6 = (bf16[320,768]{1,0:T(8,128)(2,1)S(1)}, bf16[320,768]{1,0:T(8,128)(2,1)}, u32[]{:S(2)}) copy-start(bf16[320,768]{1,0:T(8,128)(2,1)} %param.7) | copy-start | bytes 1474564
  6.5 26.5 %copy-start.5 = (bf16[320,768]{1,0:T(8,128)(2,1)S(1)}, bf16[320,768]{1,0:T(8,128)(2,1)}, u32[]{:S(2)}) copy-start(bf16[320,768]{1,0:T(8,128)(2,1)} %param.8) | copy-start | bytes 1474564
  12.5 62.0 %all-to-all-start.1 = ((s32[128,4,1]{1,2,0:T(1,128)}), s32[128,4,1]{1,2,0:T(1,128)S(1)}, u32[]{:S(2)}, u32[]{:S(2)}) async-start(s32[128,4,1]{1,2,0:T(1,128)} %bitcast.7), calls=%async_computation.1 | async-start | bytes 131072 | tf_op jit(solution)/shard_map/all_to_all | solution.py:40
  74.5 16.7 %copy-start.9 = (s32[2560,3]{0,1:T(4,128)S(1)}, s32[2560,3]{0,1:T(4,128)}, u32[]{:S(2)}) copy-start(s32[2560,3]{0,1:T(4,128)} %param.10) | copy-start | bytes 92164
  74.5 157.1 %all-to-all-start = ((bf16[512,3,768]{2,1,0:T(4,128)(2,1)}), bf16[512,3,768]{2,1,0:T(4,128)(2,1)S(1)}, u32[]{:S(2)}, u32[]{:S(2)}) async-start(bf16[512,3,768]{2,1,0:T(4,128)(2,1)} %scatter_fusion), calls=%async_computation | async-start | bytes 6291456 | tf_op jit(solution)/shard_map/all_to_all | solution.py:33
  94.4 6.0 copy-start.10
  102.7 4.5 copy-start.11
  102.7 4.5 copy-start.12
  102.7 4.5 copy-start.13
  231.6 7.9 %copy-start = (bf16[512,3,768]{2,1,0:T(4,128)(2,1)}, bf16[512,3,768]{2,1,0:T(4,128)(2,1)S(1)}, u32[]{:S(2)}) copy-start(bf16[512,3,768]{2,1,0:T(4,128)(2,1)S(1)} %all-to-all-done) | copy-start | bytes 7077892
  244.5 14.6 %copy-start.1 = (bf16[512,3,768]{2,1,0:T(4,128)(2,1)S(1)}, bf16[512,3,768]{2,1,0:T(4,128)(2,1)}, u32[]{:S(2)}) copy-start(bf16[512,3,768]{2,1,0:T(4,128)(2,1)} %copy-done) | copy-start | bytes 7077892
  244.5 301.2 %all-to-all-start.2 = ((bf16[128,16,2,768]{3,1,2,0:T(8,128)(2,1)}), bf16[128,16,2,768]{3,1,2,0:T(8,128)(2,1)}, u32[]{:S(2)}, u32[]{:S(2)}) async-start(bf16[128,16,2,768]{3,1,2,0:T(8,128)(2,1)} %gather_fusion.1), calls=%async_computation.2 | async-start | bytes 12582912 | tf_op jit(solution)/shard_map/all_to_all | solution.py:66
  256.6 367.5 %all-gather.2.cloned.1.call-start = ((), (), s32[]{:S(2)}) async-start(), calls=%async_computation.5 | async-start | bytes 4755456 | tf_op jit(solution)/shard_map/all_gather | solution.py:95
  260.8 14.2 %copy-start.2 = (bf16[320,2,768]{2,1,0:T(2,128)(2,1)S(1)}, bf16[320,2,768]{2,1,0:T(2,128)(2,1)}, u32[]{:S(2)}) copy-start(bf16[320,2,768]{2,1,0:T(2,128)(2,1)} %gather_fusion) | copy-start | bytes 2949124
  557.1 1.9 copy-start.3
  559.0 3.6 copy-start.4
  559.0 3.6 copy-start.8
  567.9 53.9 %all-to-all-start.3 = ((bf16[128,4,768]{2,1,0:T(4,128)(2,1)}), bf16[128,4,768]{2,1,0:T(4,128)(2,1)S(1)}, u32[]{:S(2)}, u32[]{:S(2)}) async-start(bf16[128,4,768]{2,1,0:T(4,128)(2,1)} %all_to_all.24), calls=%async_computation.3 | async-start | bytes 1572864 | tf_op jit(solution)/shard_map/all_to_all | solution.py:91
  580.3 79.8 %reduce-scatter.2.cloned.1.call-start = ((), (), s32[]{:S(2)}) async-start(), calls=%async_computation.6 | async-start | bytes 2457600 | tf_op jit(solution)/shard_map/reduce_scatter | solution.py:98
Sparse Core Ops, SparseCore 0:
  260.4 205.0 all-gather.1
  629.6 30.5 reduce-scatter.1
where the time goes:
time: 676 us; the launch traced here: 667 us
  waiting for transfers between devices  426 us (63%)
  local copies, waits for them, and re-layouts  146 us (22%)
  starting transfers between devices  62 us (9%)
  between operations  14.2 us (2%)
  matrix products  10.8 us (2%)
  other arithmetic  7.46 us (1%)
    all_to_all x1, waiting for transfers between devices, shards(): lax.all_to_all(cluster_blocks[pick], 'clu', split_axis=0, concat_axis=0,...  265 us
    all_to_all x1, waiting for transfers between devices, shards(): lax.all_to_all(jnp.zeros((groups * token_slots,) + rows.shape[1:], rows.d...  88.9 us
    all_to_all x1, waiting for transfers between devices, shards(): lax.all_to_all(padded[destination], 'clu', split_axis=0, concat_axis=0, t...  41.3 us
    scatter x1, local copies, waits for them, and re-layouts, shards(): jnp.zeros((groups * token_slots,) + rows.shape[1:], rows.dtype).at[slot]  37.5 us
    reduce_scatter x1, waiting for transfers between devices, shards(): lax.psum_scatter(partial_value.astype(jnp.bfloat16), 'head', scatter_dime...  30.7 us
    scatter x1, local copies, waits for them, and re-layouts, shards(): pick = jnp.zeros((groups * block_slots,), jnp.int32).at[target.reshape(-1...  28.6 us
    all_to_all x1, starting transfers between devices, shards(): lax.all_to_all(tags, 'clu', split_axis=0, concat_axis=0, tiled=True)  20.6 us
    all_to_all x1, starting transfers between devices, shards(): lax.all_to_all(jnp.zeros((groups * token_slots,) + rows.shape[1:], rows.d...  16.6 us
  transfers between devices with their start and end apart: 6, of which 4 were waited for; matrix products, arithmetic and copies ran while one was open for 21% of the time, Pallas kernels for 0%

commit v1 on v0

v1 whole, which is shorter than its diff:
```python
import functools
import math

import jax
import jax.numpy as jnp
from jax import lax
from jax.experimental import pallas as pl
from jax.experimental.pallas import tpu as pltpu
from jax.sharding import PartitionSpec as P

HD = 128
CSIZE = 16
PLANE = 8
SUBS = 4
MESH = pl.DeviceIdType.MESH
F32 = jnp.float32
BF16 = jnp.bfloat16


def ring_kernel(planes, pick_ref, kv_ref, out_ref, *rest):
    half = planes // 2
    ups = (kv_ref,) + rest[: half - 1]
    downs = (kv_ref,) + rest[half - 1 : 2 * half - 2]
    last = rest[2 * half - 2]
    stage, up_send, down_send, ring_recv, side_send, side_recv = rest[2 * half - 1 :]
    me = lax.axis_index("clu")
    z, i = me // PLANE, me % PLANE
    above = lax.rem(z + 1, planes) * PLANE + i
    below = lax.rem(z + planes - 1, planes) * PLANE + i
    step = kv_ref.shape[0] // SUBS

    def peer(j):
        return z * PLANE + lax.rem(i + j, PLANE)

    barrier = pltpu.get_barrier_semaphore()
    others = [above, below] + [peer(j) for j in range(1, PLANE)]
    for other in others:
        pl.semaphore_signal(barrier, inc=1, device_id={"clu": other}, device_id_type=MESH)
    pl.semaphore_wait(barrier, len(others))

    def ring(d, s, up):
        held = ups if up else downs
        target = last if d == half else held[d]
        rows = pl.ds(s * step, step)
        index = d if up or d == half else planes - d
        return pltpu.make_async_remote_copy(
            src_ref=held[d - 1].at[rows],
            dst_ref=target.at[rows],
            send_sem=(up_send if up else down_send).at[d - 1, s],
            recv_sem=ring_recv.at[index, s],
            device_id={"clu": above if up else below},
            device_id_type=MESH,
        )

    def travels(d, s, up):
        return d < half or (d == half and (s < SUBS // 2) == up)

    def side(k, j, source_slot):
        return pltpu.make_async_remote_copy(
            src_ref=stage.at[k * (PLANE - 1) + j - 1],
            dst_ref=out_ref.at[k * PLANE + source_slot],
            send_sem=side_send.at[k, j - 1],
            recv_sem=side_recv.at[k, source_slot],
            device_id={"clu": peer(j)},
            device_id_type=MESH,
        )

    def spread(k, held):
        out_ref[k * PLANE + i] = held[pick_ref[k * PLANE]]
        for j in range(1, PLANE):
            stage[k * (PLANE - 1) + j - 1] = held[pick_ref[k * PLANE + j]]
            side(k, j, i).start()

    for s in range(SUBS):
        ring(1, s, True).start()
        ring(1, s, False).start()
    spread(0, kv_ref)
    for d in range(1, half + 1):
        for s in range(SUBS):
            for up in (True, False):
                if travels(d, s, up):
                    ring(d, s, up).wait_recv()
                    if travels(d + 1, s, up):
                        ring(d + 1, s, up).start()
        if d < half:
            spread(d, ups[d])
            spread(planes - d, downs[d])
        else:
            spread(d, last)

    for d in range(1, half + 1):
        for s in range(SUBS):
            for up in (True, False):
                if travels(d, s, up):
                    ring(d, s, up).wait_send()

    def finish(k, carry):
        for j in range(1, PLANE):
            side(k, j, i).wait_send()
            side(k, j, lax.rem(i + PLANE - j, PLANE)).wait_recv()
        return carry

    lax.fori_loop(0, planes, finish, 0)


def ring_fetch(picks, kv, groups):
    planes = groups // PLANE
    block = kv.shape[1:]
    return pl.pallas_call(
        functools.partial(ring_kernel, planes),
        out_shape=jax.ShapeDtypeStruct((groups,) + block, kv.dtype),
        in_specs=[
            pl.BlockSpec(memory_space=pltpu.SMEM),
            pl.BlockSpec(memory_space=pltpu.VMEM),
        ],
        out_specs=pl.BlockSpec(memory_space=pltpu.VMEM),
        scratch_shapes=[pltpu.VMEM(kv.shape, kv.dtype)] * (planes - 1)
        + [
            pltpu.VMEM((planes * (PLANE - 1),) + block, kv.dtype),
            pltpu.SemaphoreType.DMA((planes // 2, SUBS)),
            pltpu.SemaphoreType.DMA((planes // 2, SUBS)),
            pltpu.SemaphoreType.DMA((planes, SUBS)),
            pltpu.SemaphoreType.DMA((planes, PLANE - 1)),
            pltpu.SemaphoreType.DMA((planes, PLANE)),
        ],
        compiler_params=pltpu.CompilerParams(
            collective_id=0, has_side_effects=True, vmem_limit_bytes=44 * 2**20
        ),
        cost_estimate=pl.CostEstimate(flops=0, bytes_accessed=2**25, transcendentals=0),
        name="ring_fetch",
    )(picks, kv)


def attend_kernel(listed, loc_ref, q_ref, kv_ref, far_ref, o_ref):
    features = q_ref.shape[2]
    heads = features // HD
    keys = (1 + listed) * CSIZE
    scale = 1.0 / math.sqrt(HD)
    row_cluster = lax.broadcasted_iota(jnp.int32, (2 * CSIZE, 2 * keys), 0) // CSIZE
    key_cluster = lax.broadcasted_iota(jnp.int32, (2 * CSIZE, 2 * keys), 1) // keys
    own = row_cluster == key_cluster

    def body(pair, carry):
        tiles = []
        for c in (2 * pair, 2 * pair + 1):
            tiles.append((kv_ref, c))
            for p in range(listed):
                tiles.append((far_ref, loc_ref[c * listed + p]))
        for h in range(heads):
            q = jnp.concatenate([q_ref[2 * pair + n, :, h * HD : (h + 1) * HD] for n in range(2)], axis=0)
            k = jnp.concatenate([ref[at, :, h * HD : (h + 1) * HD] for ref, at in tiles], axis=0)
            v = jnp.concatenate(
                [ref[at, :, features + h * HD : features + (h + 1) * HD] for ref, at in tiles], axis=0
            )
            scores = lax.dot_general(q, k, (((1,), (1,)), ((), ())), preferred_element_type=F32) * scale
            scores = jnp.where(own, scores, -jnp.inf)
            powers = jnp.exp(scores - jnp.max(scores, axis=-1, keepdims=True))
            weights = (powers / jnp.sum(powers, axis=-1, keepdims=True)).astype(BF16)
            result = jnp.dot(weights, v, preferred_element_type=F32).astype(BF16)
            for n in range(2):
                o_ref[2 * pair + n, :, h * HD : (h + 1) * HD] = result[n * CSIZE : (n + 1) * CSIZE]
        return carry

    lax.fori_loop(0, q_ref.shape[0] // 2, body, 0)


def attend(loc, q, kv, far, listed):
    return pl.pallas_call(
        functools.partial(attend_kernel, listed),
        out_shape=jax.ShapeDtypeStruct(q.shape, q.dtype),
        in_specs=[
            pl.BlockSpec(memory_space=pltpu.SMEM),
            pl.BlockSpec(memory_space=pltpu.VMEM),
            pl.BlockSpec(memory_space=pltpu.VMEM),
            pl.BlockSpec(memory_space=pltpu.VMEM),
        ],
        out_specs=pl.BlockSpec(memory_space=pltpu.VMEM),
        compiler_params=pltpu.CompilerParams(vmem_limit_bytes=32 * 2**20),
        cost_estimate=pl.CostEstimate(flops=2**27, bytes_accessed=2**23, transcendentals=2**19),
        name="attend",
    )(loc, q, kv, far)


def onehot(index, count):
    return (jnp.arange(count, dtype=jnp.int32)[:, None] == index[None, :]).astype(BF16)


def exact(a, b):
    return jnp.dot(a, b, preferred_element_type=F32)


def shards(query, key, value, labels, partners, out_weight):
    groups = lax.axis_size("clu")
    device = lax.axis_index("clu")
    tokens, features = query.shape
    per_device = tokens // CSIZE
    listed = partners.shape[1]
    quota = (3 * tokens + 2 * groups - 1) // (2 * groups)
    slots = groups * quota
    planes = groups // PLANE
    z, i = device // PLANE, device % PLANE

    owner = labels // per_device
    before = jnp.arange(tokens)[None, :] < jnp.arange(tokens)[:, None]
    rank = jnp.sum((owner[:, None] == owner[None, :]) & before, axis=1, dtype=jnp.int32)
    slot = owner * quota + rank
    packer = onehot(slot, slots)
    rows = jnp.concatenate([key, value, query], axis=1)
    packed = exact(packer, rows).astype(BF16).reshape(groups, quota, 3 * features)
    arrived = lax.all_to_all(packed, "clu", split_axis=0, concat_axis=0, tiled=True)
    arrived = arrived.reshape(slots, 3 * features)

    all_labels = lax.all_gather(labels, "clu").reshape(groups, tokens)
    mine = all_labels // per_device == device
    upto = (jnp.arange(tokens)[:, None] <= jnp.arange(tokens)[None, :]).astype(BF16)
    order = exact(mine.astype(BF16), upto).astype(jnp.int32) - 1
    local = jnp.where(mine, all_labels - device * per_device + 1, 0)
    tags = jnp.stack(
        [jnp.sum(jnp.where(order == r, local, 0), axis=1) for r in range(quota)], axis=1
    ).reshape(slots) - 1
    earlier = jnp.arange(slots)[None, :] < jnp.arange(slots)[:, None]
    position = jnp.sum((tags[:, None] == tags[None, :]) & earlier, axis=1, dtype=jnp.int32)
    destination = jnp.where(tags >= 0, tags * CSIZE + position, -1)
    placer = onehot(destination, tokens)
    placed = exact(placer, arrived).astype(BF16)
    kv = placed[:, : 2 * features].reshape(per_device, CSIZE, 2 * features)
    queries = placed[:, 2 * features :].reshape(per_device, CSIZE, features)

    wanted = partners.reshape(groups, per_device * listed)
    plane = lax.dynamic_slice_in_dim(wanted, z * PLANE, PLANE, 0)
    plane = jnp.take(plane, (i + jnp.arange(PLANE)) % PLANE, axis=0)
    source = (z - jnp.arange(planes)) % planes * PLANE + i
    hit = plane[None] // per_device == source[:, None, None]
    picks = jnp.sum(jnp.where(hit, plane[None] - source[:, None, None] * per_device, 0), axis=2)
    my_list = lax.dynamic_slice_in_dim(wanted, device, 1, 0)[0]
    from_group = my_list // per_device
    location = (z - from_group // PLANE) % planes * PLANE + from_group % PLANE

    far = ring_fetch(picks.reshape(-1).astype(jnp.int32), kv, groups)
    attended = attend(location.astype(jnp.int32), queries, kv, far, listed).reshape(tokens, features)

    outgoing = exact(placer.T, attended).astype(BF16).reshape(groups, quota, features)
    returned = lax.all_to_all(outgoing, "clu", split_axis=0, concat_axis=0, tiled=True)
    token_rows = exact(packer.T, returned.reshape(slots, features)).astype(BF16)
    partial_value = exact(token_rows, lax.all_gather(out_weight, "clu", axis=1, tiled=True))
    return lax.psum_scatter(partial_value.astype(BF16), "head", scatter_dimension=1, tiled=True)


def solution(mesh):
    return jax.shard_map(
        shards,
        mesh=mesh,
        in_specs=(
            P("clu", "head"),
            P("clu", "head"),
            P("clu", "head"),
            P("clu"),
            P(),
            P("head", "clu"),
        ),
        out_specs=P("clu", "head"),
        check_vma=False,
    )
```

time: 676 us -> 702 us (1.038); the launches traced: 667 us -> 701 us
  Pallas kernels: 0 us -> 210 us
  local copies, waits for them, and re-layouts: 146 us -> 11.8 us
  blocking collectives: 0 us -> 50.2 us
  waiting for transfers between devices: 426 us -> 378 us
  starting transfers between devices: 62 us -> 20.8 us
    all_to_all x4 -> x1, waiting for transfers between devices: 395 us -> 0.01 us  [shards(): lax.all_to_all(packed, 'clu', split_axis=0, concat_axis=0, tiled=True)]
    unnamed x2 -> x4, waiting for transfers between devices: 0.53 us -> 347 us
    pallas_call x0 -> x2, Pallas kernels: none -> 210 us  [the longest x1 190 us: ring_fetch(): pl.pallas_call(functools.partial(ring_kernel, planes), out_shape=jax.Shap...]
    scatter x4 -> x0, local copies, waits for them, and re-layouts: 72.1 us -> none  [the longest x1 37.5 us: shards(): jnp.zeros((groups * token_slots,) + rows.shape[1:], rows.dtype).at[slot]]
    all_to_all x0 -> x1, blocking collectives: none -> 50.2 us  [shards(): lax.all_to_all(outgoing, 'clu', split_axis=0, concat_axis=0, tiled=True)]
    all_to_all x4 -> x1, starting transfers between devices: 61.7 us -> 20.7 us  [shards(): lax.all_to_all(packed, 'clu', split_axis=0, concat_axis=0, tiled=True)]
    gather x7 -> x1, local copies, waits for them, and re-layouts: 29.4 us -> 0.56 us  [shards(): plane = jnp.take(plane, (i + jnp.arange(PLANE)) % PLANE, axis=0)]
    concatenate x7 -> x0, local copies, waits for them, and re-layouts: 9.44 us -> none  [the longest x3 5.48 us: shards(): jnp.concatenate([cluster_blocks[:, :, 0], listed_blocks[:, :, 0]], axis=1)]
  transfers between devices with their start and end apart: 6 -> 4, of which waited for: 4 -> 2; matrix products, arithmetic and copies ran while one was open for 21% -> 2% of each run, Pallas kernels for 0% -> 30%
where the time goes in v1:
time: 702 us; the launch traced here: 701 us
  waiting for transfers between devices  378 us (54%)
  Pallas kernels  210 us (30%)
  blocking collectives  50.2 us (7%)
  starting transfers between devices  20.8 us (3%)
  between operations  14 us (2%)
  matrix products  12 us (2%)
  local copies, waits for them, and re-layouts  11.8 us (2%)
    unnamed x4, waiting for transfers between devices  347 us
    pallas_call x1, Pallas kernels, ring_fetch(): pl.pallas_call(functools.partial(ring_kernel, planes), out_shape=jax.Shap...  190 us
    all_to_all x1, blocking collectives, shards(): lax.all_to_all(outgoing, 'clu', split_axis=0, concat_axis=0, tiled=True)  50.2 us
    reduce_scatter x1, waiting for transfers between devices, shards(): lax.psum_scatter(partial_value.astype(BF16), 'head', scatter_dimension=1,...  30.7 us
    pallas_call x1, Pallas kernels, attend(): pl.pallas_call(functools.partial(attend_kernel, listed), out_shape=jax.Sh...  20.7 us
    all_to_all x1, starting transfers between devices, shards(): lax.all_to_all(packed, 'clu', split_axis=0, concat_axis=0, tiled=True)  20.7 us
  transfers between devices with their start and end apart: 4, of which 2 were waited for; matrix products, arithmetic and copies ran while one was open for 2% of the time, Pallas kernels for 30%

profile of v1, /device:TPU:1, one launch (start us, length us, event | category | flops | bytes accessed | tf_op | source)
XLA Modules:
  0.0 701.4 jit_solution(13155776262102929707)
XLA Ops:
  6.5 0.7 add_select_fusion.2
  7.2 0.2 convert_reduce_fusion.1
  7.4 0.7 multiply_add_fusion
  8.2 2.7 convolution_convert_fusion
  10.9 2.2 reshape.177
  13.0 20.7 %all-to-all-start = ((bf16[128,4,2304]{2,1,0:T(4,128)(2,1)}), bf16[128,4,2304]{2,1,0:T(4,128)(2,1)S(1)}, u32[]{:S(2)}, u32[]{:S(2)}) async-start(bf16[128,4,2304]{2,1,0:T(4,128)(2,1)} %reshape.177), calls=%async_computation | async-start | bytes 4718592 | tf_op jit(solution)/shard_map/all_to_all | solution.py:210
  33.7 0.0 all-reduce.3.cloned.1.call-start
  33.8 1.3 dynamic-slice
  35.8 0.3 dynamic-update-slice
  36.0 0.7 copy-done
  36.7 0.0 all-reduce.3.cloned.1.call-update
  36.7 0.0 all-gather.3.cloned.1.call-start
  36.8 0.7 all-gather.3.cloned.1.call-update
  37.5 0.0 reduce-scatter.2.cloned.1.call-start
  37.5 0.0 copy-done.1
  37.6 1.5 copy.19
  39.1 1.7 reshape.176
  40.8 0.6 gather_fusion
  41.4 0.1 add_select_fusion.1
  41.5 0.4 select_reduce_fusion.4
  41.9 0.1 reshape.181.pick_ref
  42.1 346.3 %all-reduce.3.cloned.1.call-done = s32[40960]{0:T(1024)} async-done(((s32[40960]{0:T(1024)}), s32[40960]{0:T(1024)}) %all-reduce.3.cloned.1.call-update) | async-done | bytes 163856
  388.4 1.0 subtract_add_fusion
  389.3 0.1 reshape.198
  389.4 0.1 copy.14
  389.5 0.1 reshape.206
  389.7 0.1 copy.17
  389.8 1.0 fusion.14
  390.8 0.1 reshape.207
  390.9 0.1 copy.15
  391.1 0.4 select_reduce_fusion.3
  391.5 0.1 copy.18
  391.6 0.1 sub.85
  391.7 0.3 convert_reduce_fusion
  392.0 0.0 all-to-all-done
  392.0 2.2 reshape.178
  394.1 2.6 convolution_convert_fusion.2
  396.7 0.1 slice.11
  396.9 189.6 %ring_fetch.1.far_ref = bf16[128,16,1536]{2,1,0:T(8,128)(2,1)S(1)} custom-call(s32[128]{0:T(128)S(1)} %reshape.181.pick_ref, bf16[20,16,1536]{2,1,0:T(8,128)(2,1)S(1)} %bitcast.22), custom_call_target="tpu_custom_call" | custom-call | bytes 33554432 | tf_op jit(solution)/shard_map/ring_fetch/pallas_call | solution.py:109
  586.5 20.7 %attend.1 = bf16[20,16,768]{2,1,0:T(8,128)(2,1)S(1)} custom-call(s32[60]{0:T(128)S(1)} %fusion.17.loc_ref, bf16[20,16,768]{2,1,0:T(8,128)(2,1)S(1)} %bitcast.24, bf16[20,16,1536]{2,1,0:T(8,128)(2,1)S(1)} %bitcast.23, bf16[128,16,1536]{2,1,0:T(8,128)(2,1)S(1)} %ring_fetch.1.far_ref), custom_call_target="tpu_custom_call" | custom-call | flops 134217728 | bytes 8388608 | tf_op jit(solution)/shard_map/attend/pallas_call | solution.py:168
  607.2 0.7 convolution_convert_fusion.3
  607.9 0.2 reshape.183
  608.1 50.2 %all_to_all.10 = bf16[128,4,768]{2,1,0:T(4,128)(2,1)S(1)} all-to-all(bf16[128,4,768]{2,1,0:T(4,128)(2,1)S(1)} %reshape.183), channel_id=1, replica_groups=mesh['clu'=128,'head'=4] {'clu'}, dimensions={0} | all-to-all | bytes 1572864 | tf_op jit(solution)/shard_map/all_to_all | solution.py:243
  658.3 0.2 reshape.184
  658.5 0.0 all-gather.3.cloned.1.call-done
  658.5 5.7 convolution_convert_fusion.1
  664.1 0.0 reduce-scatter.2.cloned.1.call-update
  664.2 30.7 %reduce-scatter.2.cloned.1.call-done = bf16[320,768]{1,0:T(8,128)(2,1)} async-done(((bf16[320,3072]{1,0:T(8,128)(2,1)}), bf16[320,768]{1,0:T(8,128)(2,1)}) %reduce-scatter.2.cloned.1.call-update) | async-done | bytes 491536 | tf_op jit(solution)/shard_map/reduce_scatter | solution.py:246
  (14 shorter events, 0.2 us)
Async XLA Ops:
  13.0 22.7 %copy-start.2 = (s32[320]{0:T(512)S(1)}, s32[320]{0:T(512)}, u32[]{:S(2)}) copy-start(s32[320]{0:T(512)} %param.9) | copy-start | bytes 3844
  13.0 24.5 %copy-start.1 = (s32[2560,3]{0,1:T(4,128)S(1)}, s32[2560,3]{0,1:T(4,128)}, u32[]{:S(2)}) copy-start(s32[2560,3]{0,1:T(4,128)} %param.10) | copy-start | bytes 92164
  13.0 378.9 %all-to-all-start = ((bf16[128,4,2304]{2,1,0:T(4,128)(2,1)}), bf16[128,4,2304]{2,1,0:T(4,128)(2,1)S(1)}, u32[]{:S(2)}, u32[]{:S(2)}) async-start(bf16[128,4,2304]{2,1,0:T(4,128)(2,1)} %reshape.177), calls=%async_computation | async-start | bytes 4718592 | tf_op jit(solution)/shard_map/all_to_all | solution.py:210
  33.7 354.6 %all-reduce.3.cloned.1.call-start = ((), (), s32[]{:S(2)}) async-start(), calls=%async_computation.5 | async-start | bytes 327680
  36.0 0.7 copy-start
  36.7 621.8 %all-gather.3.cloned.1.call-start = ((), (), s32[]{:S(2)}) async-start(), calls=%async_computation.3 | async-start | bytes 4755456 | tf_op jit(solution)/shard_map/all_gather | solution.py:245
  37.5 657.4 %reduce-scatter.2.cloned.1.call-start = ((), (), s32[]{:S(2)}) async-start(), calls=%async_computation.4 | async-start | bytes 2457600 | tf_op jit(solution)/shard_map/reduce_scatter | solution.py:246
Sparse Core Ops, SparseCore 0:
  38.0 350.2 all-reduce.2
  391.4 144.1 all-gather.2
  664.3 30.4 reduce-scatter.1

commit v2 on v1

--- a/solution.py
+++ b/solution.py
@@ -131,13 +131,157 @@
     )(picks, kv)
 
 
+def exchange_kernel(planes, labels_ref, block_ref, out_ref, all_ref, send, recv, tag_send, tag_recv, side_send, side_recv, own):
+    me = lax.axis_index("clu")
+    z, i = me // PLANE, me % PLANE
+    half = planes // 2
+    hops = [half]
+    for d in range(half - 1, 0, -1):
+        hops += [-d, d]
+
+    def at(dz, j):
+        return lax.rem(z + dz + planes, planes) * PLANE + lax.rem(i + j + PLANE, PLANE)
+
+    barrier = pltpu.get_barrier_semaphore()
+
+    def greet(r, carry):
+        other = lax.rem(me + r, planes * PLANE)
+        pl.semaphore_signal(barrier, inc=1, device_id={"clu": other}, device_id_type=MESH)
+        return carry
+
+    lax.fori_loop(1, planes * PLANE, greet, 0)
+    pl.semaphore_wait(barrier, planes * PLANE - 1)
+
+    def copy(to, source):
+        return pltpu.make_async_remote_copy(
+            src_ref=block_ref.at[to],
+            dst_ref=out_ref.at[source],
+            send_sem=send.at[to],
+            recv_sem=recv.at[source],
+            device_id={"clu": to},
+            device_id_type=MESH,
+        )
+
+    def tag(dz, source):
+        return pltpu.make_async_remote_copy(
+            src_ref=labels_ref,
+            dst_ref=all_ref.at[i, source],
+            send_sem=tag_send.at[dz % planes],
+            recv_sem=tag_recv.at[source],
+            device_id={"clu": at(dz, 0)},
+            device_id_type=MESH,
+        )
+
+    def side(j, source):
+        return pltpu.make_async_remote_copy(
+            src_ref=all_ref.at[i],
+            dst_ref=all_ref.at[source],
+            send_sem=side_send.at[j],
+            recv_sem=side_recv.at[source],
+            device_id={"clu": at(0, j)},
+            device_id_type=MESH,
+        )
+
+    if labels_ref is not None:
+        for dz in hops:
+            tag(dz, z).start()
+
+    def start(j, carry):
+        for dz in hops:
+            copy(at(dz, j), me).start()
+        return carry
+
+    def start_side(j, carry):
+        copy(at(0, j), me).start()
+        return carry
+
+    lax.fori_loop(0, PLANE, start, 0)
+    lax.fori_loop(1, PLANE, start_side, 0)
+    mine = pltpu.make_async_copy(block_ref.at[me], out_ref.at[me], own.at[0])
+    mine.start()
+    if labels_ref is not None:
+        mine_tags = pltpu.make_async_copy(labels_ref, all_ref.at[i, z], own.at[1])
+        mine_tags.start()
+        mine_tags.wait()
+        for dz in hops:
+            tag(dz, lax.rem(z - dz + planes, planes)).wait_recv()
+        for j in range(1, PLANE):
+            side(j, i).start()
+        for j in range(1, PLANE):
+            side(j, lax.rem(i - j + PLANE, PLANE)).wait_recv()
+        for dz in hops:
+            tag(dz, z).wait_send()
+        for j in range(1, PLANE):
+            side(j, i).wait_send()
+
+    def finish(r, carry):
+        copy(lax.rem(me + r, planes * PLANE), me).wait_send()
+        copy(me, lax.rem(me + r, planes * PLANE)).wait_recv()
+        return carry
+
+    lax.fori_loop(1, planes * PLANE, finish, 0)
+    mine.wait()
+
+
+def deliver_kernel(planes, labels_ref, block_ref, out_ref, all_ref, *sems):
+    exchange_kernel(planes, labels_ref, block_ref, out_ref, all_ref, *sems)
+
+
+def give_back_kernel(planes, block_ref, out_ref, send, recv, own):
+    exchange_kernel(planes, None, block_ref, out_ref, None, send, recv, None, None, None, None, own)
+
+
+VMEM = pl.BlockSpec(memory_space=pltpu.VMEM)
+SMEM = pl.BlockSpec(memory_space=pltpu.SMEM)
+
+
+def deliver(labels, block):
+    groups = block.shape[0]
+    planes = groups // PLANE
+    dma = pltpu.SemaphoreType.DMA
+    return pl.pallas_call(
+        functools.partial(deliver_kernel, planes),
+        out_shape=(
+            jax.ShapeDtypeStruct(block.shape, block.dtype),
+            jax.ShapeDtypeStruct((PLANE, planes) + labels.shape, labels.dtype),
+        ),
+        in_specs=[VMEM, VMEM],
+        out_specs=(VMEM, VMEM),
+        scratch_shapes=[
+            dma((groups,)), dma((groups,)), dma((planes,)), dma((planes,)), dma((PLANE,)), dma((PLANE,)), dma((2,)),
+        ],
+        compiler_params=pltpu.CompilerParams(
+            collective_id=1, has_side_effects=True, vmem_limit_bytes=24 * 2**20
+        ),
+        cost_estimate=pl.CostEstimate(flops=0, bytes_accessed=2**25, transcendentals=0),
+        name="deliver",
+    )(labels, block)
+
+
+def give_back(block):
+    groups = block.shape[0]
+    dma = pltpu.SemaphoreType.DMA
+    return pl.pallas_call(
+        functools.partial(give_back_kernel, groups // PLANE),
+        out_shape=jax.ShapeDtypeStruct(block.shape, block.dtype),
+        in_specs=[VMEM],
+        out_specs=VMEM,
+        scratch_shapes=[dma((groups,)), dma((groups,)), dma((1,))],
+        compiler_params=pltpu.CompilerParams(
+            collective_id=2, has_side_effects=True, vmem_limit_bytes=16 * 2**20
+        ),
+        cost_estimate=pl.CostEstimate(flops=0, bytes_accessed=2**24, transcendentals=0),
+        name="give_back",
+    )(block)
+
+
 def attend_kernel(listed, loc_ref, q_ref, kv_ref, far_ref, o_ref):
     features = q_ref.shape[2]
     heads = features // HD
     keys = (1 + listed) * CSIZE
     scale = 1.0 / math.sqrt(HD)
-    row_cluster = lax.broadcasted_iota(jnp.int32, (2 * CSIZE, 2 * keys), 0) // CSIZE
-    key_cluster = lax.broadcasted_iota(jnp.int32, (2 * CSIZE, 2 * keys), 1) // keys
+    row_cluster = lax.broadcasted_iota(jnp.int32, (heads, 2 * CSIZE, 2 * keys), 1) // CSIZE
+    key_cluster = lax.broadcasted_iota(jnp.int32, (heads, 2 * CSIZE, 2 * keys), 2) // keys
     own = row_cluster == key_cluster
 
     def body(pair, carry):
@@ -146,17 +290,19 @@
             tiles.append((kv_ref, c))
             for p in range(listed):
                 tiles.append((far_ref, loc_ref[c * listed + p]))
+        scores, values = [], []
         for h in range(heads):
             q = jnp.concatenate([q_ref[2 * pair + n, :, h * HD : (h + 1) * HD] for n in range(2)], axis=0)
             k = jnp.concatenate([ref[at, :, h * HD : (h + 1) * HD] for ref, at in tiles], axis=0)
+            scores.append(lax.dot_general(q, k, (((1,), (1,)), ((), ())), preferred_element_type=F32))
+        scores = jnp.where(own, jnp.stack(scores) * scale, -jnp.inf)
+        powers = jnp.exp(scores - jnp.max(scores, axis=-1, keepdims=True))
+        weights = (powers / jnp.sum(powers, axis=-1, keepdims=True)).astype(BF16)
+        for h in range(heads):
             v = jnp.concatenate(
                 [ref[at, :, features + h * HD : features + (h + 1) * HD] for ref, at in tiles], axis=0
             )
-            scores = lax.dot_general(q, k, (((1,), (1,)), ((), ())), preferred_element_type=F32) * scale
-            scores = jnp.where(own, scores, -jnp.inf)
-            powers = jnp.exp(scores - jnp.max(scores, axis=-1, keepdims=True))
-            weights = (powers / jnp.sum(powers, axis=-1, keepdims=True)).astype(BF16)
-            result = jnp.dot(weights, v, preferred_element_type=F32).astype(BF16)
+            result = jnp.dot(weights[h], v, preferred_element_type=F32).astype(BF16)
             for n in range(2):
                 o_ref[2 * pair + n, :, h * HD : (h + 1) * HD] = result[n * CSIZE : (n + 1) * CSIZE]
         return carry
@@ -203,14 +349,21 @@
     owner = labels // per_device
     before = jnp.arange(tokens)[None, :] < jnp.arange(tokens)[:, None]
     rank = jnp.sum((owner[:, None] == owner[None, :]) & before, axis=1, dtype=jnp.int32)
-    slot = owner * quota + rank
-    packer = onehot(slot, slots)
-    rows = jnp.concatenate([key, value, query], axis=1)
-    packed = exact(packer, rows).astype(BF16).reshape(groups, quota, 3 * features)
-    arrived = lax.all_to_all(packed, "clu", split_axis=0, concat_axis=0, tiled=True)
-    arrived = arrived.reshape(slots, 3 * features)
-
-    all_labels = lax.all_gather(labels, "clu").reshape(groups, tokens)
+    slot = owner * (2 * quota) + rank
+    packer = onehot(jnp.concatenate([slot, slot + quota]), 2 * slots)
+    wide = 3 * features // 2
+    rows = jnp.concatenate(
+        [
+            jnp.concatenate([key, value[:, : wide - features]], axis=1),
+            jnp.concatenate([value[:, wide - features :], query], axis=1),
+        ],
+        axis=0,
+    )
+    packed = exact(packer, rows).astype(BF16).reshape(groups, 2 * quota, wide)
+    arrived, all_labels = deliver(labels.reshape(1, tokens), packed)
+    arrived = arrived.reshape(2 * slots, wide)
+
+    all_labels = all_labels.reshape(PLANE, planes, tokens).transpose(1, 0, 2).reshape(groups, tokens)
     mine = all_labels // per_device == device
     upto = (jnp.arange(tokens)[:, None] <= jnp.arange(tokens)[None, :]).astype(BF16)
     order = exact(mine.astype(BF16), upto).astype(jnp.int32) - 1
@@ -220,11 +373,19 @@
     ).reshape(slots) - 1
     earlier = jnp.arange(slots)[None, :] < jnp.arange(slots)[:, None]
     position = jnp.sum((tags[:, None] == tags[None, :]) & earlier, axis=1, dtype=jnp.int32)
-    destination = jnp.where(tags >= 0, tags * CSIZE + position, -1)
-    placer = onehot(destination, tokens)
+    destination = jnp.where(tags >= 0, tags * CSIZE + position, -1).reshape(groups, quota)
+    nowhere = jnp.full_like(destination, -1)
+    placer = jnp.concatenate(
+        [
+            onehot(jnp.concatenate([destination, nowhere], axis=1).reshape(-1), tokens),
+            onehot(jnp.concatenate([nowhere, destination], axis=1).reshape(-1), tokens),
+        ],
+        axis=0,
+    )
     placed = exact(placer, arrived).astype(BF16)
-    kv = placed[:, : 2 * features].reshape(per_device, CSIZE, 2 * features)
-    queries = placed[:, 2 * features :].reshape(per_device, CSIZE, features)
+    kv = jnp.concatenate([placed[:tokens], placed[tokens:, : 2 * features - wide]], axis=1)
+    kv = kv.reshape(per_device, CSIZE, 2 * features)
+    queries = placed[tokens:, 2 * features - wide :].reshape(per_device, CSIZE, features)
 
     wanted = partners.reshape(groups, per_device * listed)
     plane = lax.dynamic_slice_in_dim(wanted, z * PLANE, PLANE, 0)
@@ -239,9 +400,11 @@
     far = ring_fetch(picks.reshape(-1).astype(jnp.int32), kv, groups)
     attended = attend(location.astype(jnp.int32), queries, kv, far, listed).reshape(tokens, features)
 
-    outgoing = exact(placer.T, attended).astype(BF16).reshape(groups, quota, features)
-    returned = lax.all_to_all(outgoing, "clu", split_axis=0, concat_axis=0, tiled=True)
-    token_rows = exact(packer.T, returned.reshape(slots, features)).astype(BF16)
+    halves = jnp.concatenate([attended[:, : features // 2], attended[:, features // 2 :]], axis=0)
+    outgoing = exact(placer.T, halves).astype(BF16).reshape(groups, 2 * quota, features // 2)
+    returned = give_back(outgoing).reshape(2 * slots, features // 2)
+    token_rows = exact(packer.T, returned).astype(BF16)
+    token_rows = jnp.concatenate([token_rows[:tokens], token_rows[tokens:]], axis=1)
     partial_value = exact(token_rows, lax.all_gather(out_weight, "clu", axis=1, tiled=True))
     return lax.psum_scatter(partial_value.astype(BF16), "head", scatter_dimension=1, tiled=True)
 

time: 702 us -> 436 us (0.62)
  waiting for transfers between devices: 378 us -> 31.9 us
  Pallas kernels: 210 us -> 365 us
  blocking collectives: 50.2 us -> 0 us
  starting transfers between devices: 20.8 us -> 0.04 us
    unnamed x4 -> x2, waiting for transfers between devices: 347 us -> 0.73 us
    pallas_call x0 -> x2, Pallas kernels: none -> 182 us  [the longest x1 134 us: deliver(): pl.pallas_call(functools.partial(deliver_kernel, planes), out_shape=(jax....]
    all_to_all x1 -> x0, blocking collectives: 50.2 us -> none  [shards(): lax.all_to_all(outgoing, 'clu', split_axis=0, concat_axis=0, tiled=True)]
    all_to_all x1 -> x0, starting transfers between devices: 20.7 us -> none  [shards(): lax.all_to_all(packed, 'clu', split_axis=0, concat_axis=0, tiled=True)]
    pallas_call x1, Pallas kernels: 20.7 us -> 5.6 us  [attend(): pl.pallas_call(functools.partial(attend_kernel, listed), out_shape=jax.Sh...]
    pallas_call x1, Pallas kernels: 190 us -> 178 us  [ring_fetch(): pl.pallas_call(functools.partial(ring_kernel, planes), out_shape=jax.Shap...]
  transfers between devices with their start and end apart: 4 -> 2, of which waited for: 2 -> 1; matrix products, arithmetic and copies ran while one was open for 2% -> 4% of each run, Pallas kernels for 30% -> 84%
where the time goes in v2:
time: 436 us
  Pallas kernels  365 us (84%)
  waiting for transfers between devices  31.9 us (7%)
  between operations  13.7 us (3%)
  matrix products  12.8 us (3%)
  local copies, waits for them, and re-layouts  6.99 us (2%)
  other arithmetic  4.49 us (1%)
    pallas_call x1, Pallas kernels, ring_fetch(): pl.pallas_call(functools.partial(ring_kernel, planes), out_shape=jax.Shap...  178 us
    pallas_call x1, Pallas kernels, deliver(): pl.pallas_call(functools.partial(deliver_kernel, planes), out_shape=(jax....  134 us
    pallas_call x1, Pallas kernels, give_back(): pl.pallas_call(functools.partial(give_back_kernel, groups // PLANE), out_...  48.4 us
    reduce_scatter x1, waiting for transfers between devices, shards(): lax.psum_scatter(partial_value.astype(BF16), 'head', scatter_dimension=1,...  31.2 us
    dot_general x6, matrix products, exact(): return jnp.dot(a, b, preferred_element_type=F32)  12.8 us
  transfers between devices with their start and end apart: 2, of which 1 were waited for; matrix products, arithmetic and copies ran while one was open for 4% of the time, Pallas kernels for 84%

profile of v2, /device:TPU:1, one launch (start us, length us, event | category | flops | bytes accessed | tf_op | source)
XLA Modules:
  0.0 435.5 jit_solution(8599889370775480361)
XLA Ops:
  6.5 0.7 all-gather.2.cloned.1.call-update
  7.3 0.0 reduce-scatter.2.cloned.1.call-start
  7.3 0.7 reshape.203.labels_ref
  8.0 0.7 add_select_fusion.2
  8.7 0.2 convert_reduce_fusion.1
  8.9 0.7 broadcast_add_fusion
  9.6 0.1 pad_add_fusion.3
  9.7 1.1 fusion.44
  10.8 3.3 fusion.block_ref
  14.1 133.9 %deliver.1 = (bf16[128,8,1152]{2,1,0:T(8,128)(2,1)S(1)}, s32[8,16,1,320]{3,2,1,0:T(1,128)S(1)}) custom-call(s32[1,320]{1,0:T(1,128)S(1)} %reshape.203.labels_ref, bf16[128,8,1152]{2,1,0:T(8,128)(2,1)S(1)} %fusion.block_ref), custom_call_target="tpu_custom_call" | custom-call | bytes 33554432 | tf_op jit(solution)/shard_map/deliver/pallas_call | solution.py:242
  148.0 0.5 subtract_add_fusion
  148.6 0.1 copy_bitcast_fusion
  148.7 0.1 copy.22
  148.8 0.1 copy.26
  148.9 1.0 compare_and_fusion
  149.9 0.1 copy.43
  150.0 0.1 copy.23
  150.1 0.4 select_reduce_fusion.3
  150.5 0.1 copy.27
  150.6 0.1 sub.88
  150.7 0.3 convert_reduce_fusion
  151.0 0.1 reduce_sum.71
  151.1 0.1 copy.28
  151.2 0.1 copy.35
  151.3 0.1 fusion.45
  151.4 0.1 eq.138
  151.5 0.1 eq.134
  151.6 0.2 iota_compare_fusion.3
  151.8 0.2 iota_compare_fusion.4
  152.0 1.9 convolution_convert_fusion.2
  153.9 1.1 copy-done
  155.0 1.1 slice.38
  156.2 0.4 copy.31
  156.6 0.4 reshape.205
  157.1 0.6 gather_fusion
  157.7 0.1 add_select_fusion.1
  157.8 0.4 select_reduce_fusion.4
  158.2 0.1 reshape.209.pick_ref
  158.3 0.1 pad_maximum_fusion
  158.4 177.6 %ring_fetch.1.far_ref = bf16[128,16,1536]{2,1,0:T(8,128)(2,1)S(1)} custom-call(s32[128]{0:T(128)S(1)} %reshape.209.pick_ref, bf16[20,16,1536]{2,1,0:T(8,128)(2,1)S(1)} %bitcast.50), custom_call_target="tpu_custom_call" | custom-call | bytes 33554432 | tf_op jit(solution)/shard_map/ring_fetch/pallas_call | solution.py:109
  336.0 5.6 %attend.1 = bf16[20,16,768]{2,1,0:T(8,128)(2,1)S(1)} custom-call(s32[60]{0:T(128)S(1)} %fusion.27.loc_ref, bf16[20,16,768]{2,1,0:T(8,128)(2,1)S(1)} %bitcast.52, bf16[20,16,1536]{2,1,0:T(8,128)(2,1)S(1)} %bitcast.51, bf16[128,16,1536]{2,1,0:T(8,128)(2,1)S(1)} %ring_fetch.1.far_ref), custom_call_target="tpu_custom_call" | custom-call | flops 134217728 | bytes 8388608 | tf_op jit(solution)/shard_map/attend/pallas_call | solution.py:314
  341.6 0.1 fusion.43
  341.7 1.0 fusion.12.block_ref
  342.7 48.4 %give_back.1 = bf16[128,8,384]{2,1,0:T(8,128)(2,1)S(1)} custom-call(bf16[128,8,384]{2,1,0:T(8,128)(2,1)S(1)} %fusion.12.block_ref), custom_call_target="tpu_custom_call" | custom-call | bytes 16777216 | tf_op jit(solution)/shard_map/give_back/pallas_call | solution.py:264
  391.1 0.9 fusion.13
  392.0 0.1 fusion.42
  392.1 5.4 %convolution_convert_fusion = bf16[320,3072]{1,0:T(8,128)(2,1)} fusion(bf16[768,3072]{0,1:T(8,128)(2,1)} %all-gather.2.cloned.1.call-done, bf16[320,384]{1,0:T(8,128)(2,1)S(1)} %get-tuple-element.20, bf16[320,384]{1,0:T(8,128)(2,1)S(1)} %get-tuple-element.19), kind=kOutput, calls=%fused_computation.1 | convolution fusion | flops 1511915520 | bytes 7176192 | tf_op jit(solution)/shard_map/dot_general | solution.py:335
  397.5 31.2 %reduce-scatter.2.cloned.1.call-done = bf16[320,768]{1,0:T(8,128)(2,1)} async-done(((bf16[320,3072]{1,0:T(8,128)(2,1)}), bf16[320,768]{1,0:T(8,128)(2,1)}) %reduce-scatter.2.cloned.1.call-update) | async-done | bytes 491536 | tf_op jit(solution)/shard_map/reduce_scatter | solution.py:409
  (17 shorter events, 0.2 us)
Async XLA Ops:
  6.5 385.6 %all-gather.2.cloned.1.call-start = ((), (), s32[]{:S(2)}) async-start(), calls=%async_computation.1 | async-start | bytes 4755456 | tf_op jit(solution)/shard_map/all_gather | solution.py:408
  7.3 421.4 %reduce-scatter.2.cloned.1.call-start = ((), (), s32[]{:S(2)}) async-start(), calls=%async_computation.2 | async-start | bytes 2457600 | tf_op jit(solution)/shard_map/reduce_scatter | solution.py:409
  153.8 1.1 copy-start
  153.8 2.4 copy-start.1
  155.0 3.3 slice-start
Sparse Core Ops, SparseCore 0:
  10.4 172.6 all-gather.1
  397.6 30.9 reduce-scatter.1

commit v3 on v0

v3 whole, which is shorter than its diff:
```python
import functools
import math

import jax
import jax.numpy as jnp
import numpy as np
from jax import lax
from jax.experimental import pallas as pl
from jax.experimental.pallas import tpu as pltpu
from jax.sharding import PartitionSpec as P

HD = 128
CSIZE = 16
PLANE = 8
SUBS = 4
GROUPS = (4, 2)
LANES = 128
MESH = pl.DeviceIdType.MESH
F32 = jnp.float32
BF16 = jnp.bfloat16
VMEM = pl.BlockSpec(memory_space=pltpu.VMEM)
SMEM = pl.BlockSpec(memory_space=pltpu.SMEM)


def drain(ref, count, sem):
    some = ref.at[pl.ds(0, count)]
    pltpu.make_async_copy(some, some, sem).wait()


def exact(a, b):
    return jnp.dot(a, b, preferred_element_type=F32)


class Ring:
    def __init__(self, planes, z, i, pick, kv, out, ups, downs, packs, near, far, stage, sems):
        self.planes, self.half, self.full = planes, planes // 2, planes // 2 - 2
        self.z, self.i = z, i
        self.above = lax.rem(z + 1, planes) * PLANE + i
        self.below = lax.rem(z + planes - 1, planes) * PLANE + i
        self.pick, self.kv, self.out = pick, kv, out
        self.ups, self.downs = (kv,) + ups, (kv,) + downs
        self.packs, self.near, self.far, self.stage = packs, near, far, stage
        self.ring_send, self.ring_recv, self.pack_send, self.pack_recv, self.side_send, self.side_recv = sems
        self.step = kv.shape[0] // SUBS
        self.part = PLANE // 2

    def send_on(self, src, dst, send, recv, up):
        return pltpu.make_async_remote_copy(
            src_ref=src,
            dst_ref=dst,
            send_sem=send,
            recv_sem=recv,
            device_id={"clu": self.above if up else self.below},
            device_id_type=MESH,
        )

    def hop(self, d, s, up):
        held = self.ups if up else self.downs
        rows = pl.ds(s * self.step, self.step)
        n = 0 if up else 1
        return self.send_on(
            held[d - 1].at[rows], held[d].at[rows], self.ring_send.at[n, d - 1, s], self.ring_recv.at[n, d - 1, s], up
        )

    def pack(self, at, up):
        n = 0 if up else 1
        rows = pl.ds(0, self.part) if at == 0 else pl.ds(self.part, PLANE)
        return self.send_on(
            self.packs.at[n, rows], self.near.at[n, rows], self.pack_send.at[n, at], self.pack_recv.at[n, at], up
        )

    def pack_on(self, up):
        n = 0 if up else 1
        return self.send_on(
            self.near.at[n, pl.ds(0, self.part)], self.far.at[n], self.pack_send.at[n, 2], self.pack_recv.at[n, 2], up
        )

    def side(self, k, j, src):
        return pltpu.make_async_remote_copy(
            src_ref=src,
            dst_ref=self.out.at[k * PLANE + self.i],
            send_sem=self.side_send,
            recv_sem=self.side_recv,
            device_id={"clu": self.z * PLANE + lax.rem(self.i + j, PLANE)},
            device_id_type=MESH,
        )

    def spread(self, k, held):
        self.out[k * PLANE + self.i] = held[self.pick[k * PLANE]]
        for j in range(1, PLANE):
            at = k * (PLANE - 1) + j - 1
            self.stage[at] = held[self.pick[k * PLANE + j]]
            self.side(k, j, self.stage.at[at]).start()

    def pass_out(self, k, j, src):
        if j == 0:
            self.out[k * PLANE + self.i] = src[...]
        else:
            self.side(k, j, src).start()

    def begin(self):
        for s in range(SUBS):
            for up in (True, False):
                self.hop(1, s, up).start()
        self.spread(0, self.kv)

    def advance(self, d):
        for s in range(SUBS):
            for up in (True, False):
                self.hop(d, s, up).wait_recv()
                if d < self.full:
                    self.hop(d + 1, s, up).start()
        if d == self.full:
            for up in (True, False):
                n = 0 if up else 1
                held = (self.ups if up else self.downs)[d]
                base = (self.planes + 2 * n) * PLANE
                for j in range(self.part):
                    self.packs[n, j] = held[self.pick[base + n * self.part + j]]
                self.pack(0, up).start()
                for j in range(PLANE):
                    self.packs[n, self.part + j] = held[self.pick[base + PLANE + j]]
                self.pack(1, up).start()
        self.spread(d, self.ups[d])
        self.spread(self.planes - d, self.downs[d])

    def last_hops(self):
        for up in (True, False):
            self.pack(0, up).wait_recv()
            self.pack_on(up).start()
        for up in (True, False):
            n = 0 if up else 1
            self.pack(1, up).wait_recv()
            for j in range(PLANE):
                self.pass_out(self.full + 1 if up else self.planes - self.full - 1, j, self.near.at[n, self.part + j])
        for up in (True, False):
            n = 0 if up else 1
            self.pack_on(up).wait_recv()
            for j in range(self.part):
                self.pass_out(self.half, n * self.part + j, self.far.at[n, j])

    def arrive(self):
        drain(self.out, self.planes * (PLANE - 1), self.side_recv)

    def finish(self):
        for up in (True, False):
            for d in range(1, self.full + 1):
                for s in range(SUBS):
                    self.hop(d, s, up).wait_send()
            self.pack(0, up).wait_send()
            self.pack(1, up).wait_send()
            self.pack_on(up).wait_send()
        drain(self.stage, self.planes * (PLANE - 1), self.side_send)


def attend(listed, first, heads, loc_ref, q_ref, kv_ref, far_ref, o_ref):
    keys = (1 + listed) * CSIZE
    width = heads * HD
    scale = 1.0 / math.sqrt(HD)
    shape = (heads, 2 * CSIZE, 2 * keys)
    row, key = lax.broadcasted_iota(jnp.int32, shape, 1), lax.broadcasted_iota(jnp.int32, shape, 2)
    own = (row >= CSIZE) == (key >= keys)

    def body(pair, carry):
        tiles = []
        for c in (2 * pair, 2 * pair + 1):
            tiles.append((kv_ref, c))
            for p in range(listed):
                tiles.append((far_ref, loc_ref[c * listed + p]))
        scores = []
        for h in range(heads):
            at = (first + h) * HD
            q = jnp.concatenate([q_ref[2 * pair + n, :, at : at + HD] for n in range(2)], axis=0)
            k = jnp.concatenate([ref[at, :, h * HD : (h + 1) * HD] for ref, at in tiles], axis=0)
            scores.append(lax.dot_general(q, k, (((1,), (1,)), ((), ())), preferred_element_type=F32))
        scores = jnp.where(own, jnp.stack(scores) * scale, -jnp.inf)
        powers = jnp.exp(scores - jnp.max(scores, axis=-1, keepdims=True))
        weights = (powers / jnp.sum(powers, axis=-1, keepdims=True)).astype(BF16)
        for h in range(heads):
            v = jnp.concatenate([ref[at, :, width + h * HD : width + (h + 1) * HD] for ref, at in tiles], axis=0)
            o_ref[pl.ds(2 * CSIZE * pair, 2 * CSIZE), h * HD : (h + 1) * HD] = exact(weights[h], v).astype(BF16)
        return carry

    lax.fori_loop(0, q_ref.shape[0] // 2, body, 0)


def layer_kernel(planes, listed, *refs):
    (pick, loc, labels_ref, send0, send1, sendq, upto, lower, col, row, col_mask, row_mask, ret0, ret1, *rest) = refs
    (arr0, arr1, arrq, all_ref, lab, dcol, drow, q_ref, back0, back1, o0, o1, *rest) = rest
    (a2a_send, a2a_recv, tag_send, tag_recv, tag_side_send, tag_side_recv, *rest) = rest
    per_ring = len(rest) // 2
    me = lax.axis_index("clu")
    z, i = me // PLANE, me % PLANE
    half, full, total = planes // 2, planes // 2 - 2, planes * PLANE
    hops = [half]
    for d in range(half - 1, 0, -1):
        hops += [-d, d]

    rings = []
    for g in range(2):
        kv, out, *more = rest[g * per_ring : (g + 1) * per_ring]
        ups, downs, more = tuple(more[:full]), tuple(more[full : 2 * full]), more[2 * full :]
        rings.append(Ring(planes, z, i, pick, kv, out, ups, downs, *more[:4], more[4:]))

    def at(dz, j):
        return lax.rem(z + dz + planes, planes) * PLANE + lax.rem(i + j, PLANE)

    barrier = pltpu.get_barrier_semaphore()

    def greet(r, carry):
        other = lax.rem(me + r, total)
        pl.semaphore_signal(barrier, inc=1, device_id={"clu": other}, device_id_type=MESH)
        return carry

    lax.fori_loop(1, total, greet, 0)
    pl.semaphore_wait(barrier, total - 1)

    def tag(dz, source):
        return pltpu.make_async_remote_copy(
            src_ref=labels_ref,
            dst_ref=all_ref.at[i, source],
            send_sem=tag_send.at[dz % planes],
            recv_sem=tag_recv.at[source],
            device_id={"clu": at(dz, 0)},
            device_id_type=MESH,
        )

    def tag_side(j, source):
        return pltpu.make_async_remote_copy(
            src_ref=all_ref.at[i],
            dst_ref=all_ref.at[source],
            send_sem=tag_side_send.at[j],
            recv_sem=tag_side_recv.at[source],
            device_id={"clu": at(0, j)},
            device_id_type=MESH,
        )

    def exchange(n, block, landed):
        def start(to):
            pltpu.make_async_remote_copy(
                src_ref=block.at[to],
                dst_ref=landed.at[me],
                send_sem=a2a_send.at[n],
                recv_sem=a2a_recv.at[n],
                device_id={"clu": to},
                device_id_type=MESH,
            ).start()

        def far(j, carry):
            for dz in hops:
                start(at(dz, j))
            return carry

        def close(j, carry):
            start(at(0, j))
            return carry

        lax.fori_loop(0, PLANE, far, 0)
        lax.fori_loop(1, PLANE, close, 0)
        landed[me] = block[me]

    def landed_all(n, landed):
        drain(landed, total - 1, a2a_recv.at[n])

    for dz in hops:
        tag(dz, z).start()
    all_ref[i, z] = labels_ref[...]
    exchange(0, send0, arr0)
    for dz in hops:
        tag(dz, lax.rem(z - dz + planes, planes)).wait_recv()
    for j in range(1, PLANE):
        tag_side(j, i).start()
    exchange(1, send1, arr1)
    exchange(2, sendq, arrq)
    for j in range(1, PLANE):
        tag_side(j, lax.rem(i - j + PLANE, PLANE)).wait_recv()

    for zz in range(planes):
        for ii in range(PLANE):
            lab[zz * PLANE + ii : zz * PLANE + ii + 1, :] = all_ref[ii, zz]
    per_device = q_ref.shape[0]
    quota = send0.shape[1] // 2
    local = lab[...] - me * per_device
    mine = jnp.logical_and(local >= 0, local < per_device)
    order = exact(jnp.where(mine, 1.0, 0.0).astype(BF16), upto[...])
    named = jnp.where(mine, (local + 1).astype(F32), 0.0)
    lane = lax.broadcasted_iota(jnp.int32, (total, LANES), 1)
    lanef = lane.astype(F32)
    tags, marks = [], []
    for r in range(quota):
        one = jnp.sum(jnp.where(order == r + 1.0, named, 0.0), axis=1, keepdims=True)
        one = jnp.where(one > 0.0, one - 1.0, -100.0)
        tags.append(one)
        marks.append(jnp.where(lanef == one, 1.0, 0.0))
    earlier = exact(lower[...], sum(marks).astype(BF16))
    table = jnp.where(lane == 2 * quota, 1.0, 0.0)
    for r in range(quota):
        place = jnp.sum(marks[r] * earlier, axis=1, keepdims=True)
        table = jnp.where(lane == r, tags[r], jnp.where(lane == quota + r, place, table))
        earlier = earlier + marks[r]
    wide = exact(col[...], table.astype(BF16))
    tall = exact(table.T.astype(BF16), row[...])
    slots, tokens = dcol.shape[1], dcol.shape[2]
    for p in range(2):
        to = jnp.sum(wide * col_mask[p], axis=1, keepdims=True)
        rows = lax.broadcasted_iota(jnp.int32, (slots, tokens), 1).astype(F32)
        dcol[p] = jnp.where(rows == to, 1.0, 0.0).astype(BF16)
        to = jnp.sum(tall * row_mask[p], axis=0, keepdims=True)
        rows = lax.broadcasted_iota(jnp.int32, (tokens, slots), 0).astype(F32)
        drow[p] = jnp.where(rows == to, 1.0, 0.0).astype(BF16)

    def unpack(landed, target):
        width = landed.shape[2]
        for l in range(0, width, LANES):
            block = landed[:, :, l : l + LANES].astype(F32).reshape(slots, LANES).astype(BF16)
            for p in range(2):
                part = exact(drow[p], block).astype(BF16).reshape(per_device, CSIZE, LANES)
                target[:, :, p * width + l : p * width + l + LANES] = part

    def give_back(n, attended, back, ret):
        width = back.shape[2]
        for l in range(0, width, LANES):
            part = exact(dcol[0], attended[:, l : l + LANES]) + exact(dcol[1], attended[:, width + l : width + l + LANES])
            back[:, :, l : l + LANES] = part.reshape(total, 2 * quota, LANES).astype(BF16)
        exchange(n, back, ret)

    first, second = rings
    landed_all(0, arr0)
    unpack(arr0, first.kv)
    first.begin()
    for d in range(1, full + 1):
        first.advance(d)
    landed_all(1, arr1)
    unpack(arr1, second.kv)
    second.begin()
    first.last_hops()
    landed_all(2, arrq)
    unpack(arrq, q_ref)
    second.advance(1)
    first.arrive()
    attend(listed, 0, GROUPS[0], loc, q_ref, first.kv, first.out, o0)
    second.advance(2)
    give_back(3, o0, back0, ret0)
    for d in range(3, full + 1):
        second.advance(d)
    second.last_hops()
    second.arrive()
    attend(listed, GROUPS[0], GROUPS[1], loc, q_ref, second.kv, second.out, o1)
    give_back(4, o1, back1, ret1)

    for dz in hops:
        tag(dz, z).wait_send()
    for j in range(1, PLANE):
        tag_side(j, i).wait_send()
    first.finish()
    second.finish()
    for n, block in enumerate((send0, send1, sendq, back0, back1)):
        drain(block, total - 1, a2a_send.at[n])
    landed_all(3, ret0)
    landed_all(4, ret1)


def project_kernel(rows_ref, weight_ref, out_ref, sent, came, near, send, recv):
    n = lax.axis_size("head")
    x = lax.axis_index("head")
    left, right = lax.rem(x + n - 1, n), lax.rem(x + 1, n)
    width = out_ref.shape[1]
    part = width // 2

    def block(to, first, count):
        start = pl.multiple_of(to * width + first, LANES)
        return exact(rows_ref[...], weight_ref[:, pl.ds(start, count)])

    barrier = pltpu.get_barrier_semaphore()
    for other in (left, right):
        pl.semaphore_signal(barrier, inc=1, device_id={"head": other}, device_id_type=MESH)

    def copy(way, piece, src, dst):
        return pltpu.make_async_remote_copy(
            src_ref=src,
            dst_ref=dst,
            send_sem=send.at[way, piece],
            recv_sem=recv.at[way, piece],
            device_id={"head": right if way == 0 else left},
            device_id_type=MESH,
        )

    copies = [[copy(w, 0, sent.at[w, 0], near.at[w])] + [copy(w, p, sent.at[w, p], came.at[w, p - 1]) for p in (1, 2)] for w in range(2)]
    opposite = lax.rem(x + 2, n)
    for w in range(2):
        sent[w, 0] = block(opposite, w * part, part).astype(BF16)
    pl.semaphore_wait(barrier, 2)
    for w in range(2):
        copies[w][0].start()
    for w in range(2):
        sent[w, 1] = block(right if w == 0 else left, (1 - w) * part, part).astype(BF16)
        copies[w][1].start()
    summed = [block(right if w == 0 else left, w * part, part) for w in range(2)]
    for w in range(2):
        copies[w][0].wait_recv()
        sent[w, 2] = (summed[w].astype(BF16).astype(F32) + near[w].astype(F32)).astype(BF16)
        copies[w][2].start()
    own = [block(x, h * part, part).astype(BF16).astype(F32) for h in range(2)]
    for w in range(2):
        copies[w][1].wait_recv()
    for w in range(2):
        copies[w][2].wait_recv()
    for h in range(2):
        total = own[h]
        for w in range(2):
            total = total + came[w, 1 if h == w else 0].astype(F32)
        out_ref[:, h * part : (h + 1) * part] = total.astype(BF16)
    for w in range(2):
        for p in range(3):
            copies[w][p].wait_send()


def project(rows, weight, width):
    tokens = rows.shape[0]
    half = (tokens, width // 2)
    dma = pltpu.SemaphoreType.DMA
    return pl.pallas_call(
        project_kernel,
        out_shape=jax.ShapeDtypeStruct((tokens, width), BF16),
        in_specs=[VMEM, VMEM],
        out_specs=VMEM,
        scratch_shapes=[
            pltpu.VMEM((2, 3) + half, BF16),
            pltpu.VMEM((2, 2) + half, BF16),
            pltpu.VMEM((2,) + half, BF16),
            dma((2, 3)),
            dma((2, 3)),
        ],
        compiler_params=pltpu.CompilerParams(
            collective_id=1, has_side_effects=True, vmem_limit_bytes=24 * 2**20
        ),
        cost_estimate=pl.CostEstimate(flops=2**31, bytes_accessed=2**23, transcendentals=0),
        name="project",
    )(rows, weight)


def constants(groups, tokens, quota):
    slots = 2 * groups * quota
    s = np.arange(slots)
    token = np.arange(tokens)
    block = np.arange(groups)
    upto = (token[:, None] <= token[None, :]).astype(np.float32)
    lower = (block[None, :] < block[:, None]).astype(np.float32)
    col = (s[:, None] // (2 * quota) == block[None, :]).astype(np.float32)
    lane = np.arange(LANES)[None, :]
    r, half = (s % quota)[:, None], (s // quota % 2)[:, None]
    masks = []
    for p in range(2):
        masks.append(CSIZE * (lane == r) + 1.0 * (lane == quota + r) - 10000.0 * ((lane == 2 * quota) & (half != p)))
    col_mask = np.stack(masks).astype(np.float32)
    row_mask = np.ascontiguousarray(col_mask.transpose(0, 2, 1))
    as16 = lambda x: jnp.asarray(x, BF16)
    return as16(upto), as16(lower), as16(col), as16(col.T), jnp.asarray(col_mask), jnp.asarray(row_mask)


def layer(picks, location, labels, sends, groups, per_device, listed):
    planes = groups // PLANE
    full = planes // 2 - 2
    tokens = per_device * CSIZE
    quota = sends[0].shape[1] // 2
    slots = 2 * groups * quota
    dma = pltpu.SemaphoreType.DMA

    def scratch(*shape):
        return pltpu.VMEM(shape, BF16)

    widths = [heads * HD for heads in GROUPS]
    landings = [scratch(*x.shape) for x in sends]
    backs = [(groups, 2 * quota, w // 2) for w in widths]
    rings = []
    for w in widths:
        shard, block = (per_device, CSIZE, 2 * w), (CSIZE, 2 * w)
        rings += [scratch(*shard), scratch(groups, *block)]
        rings += [scratch(*shard)] * (2 * full)
        rings += [scratch(2, PLANE + PLANE // 2, *block)] * 2
        rings += [scratch(2, PLANE // 2, *block), scratch(planes * (PLANE - 1), *block)]
        rings += [dma((2, full, SUBS)), dma((2, full, SUBS)), dma((2, 3)), dma((2, 3)), dma, dma]
    return pl.pallas_call(
        functools.partial(layer_kernel, planes, listed),
        out_shape=tuple(jax.ShapeDtypeStruct(b, BF16) for b in backs),
        in_specs=[SMEM, SMEM] + [VMEM] * 10,
        out_specs=(VMEM, VMEM),
        scratch_shapes=landings
        + [
            pltpu.VMEM((PLANE, planes) + labels.shape, labels.dtype),
            pltpu.VMEM((groups, tokens), labels.dtype),
            scratch(2, slots, tokens),
            scratch(2, tokens, slots),
            scratch(per_device, CSIZE, sum(widths)),
        ]
        + [scratch(*b) for b in backs]
        + [scratch(tokens, w) for w in widths]
        + [dma((5,)), dma((5,)), dma((planes,)), dma((planes,)), dma((PLANE,)), dma((PLANE,))]
        + rings,
        compiler_params=pltpu.CompilerParams(
            collective_id=0, has_side_effects=True, vmem_limit_bytes=56 * 2**20
        ),
        cost_estimate=pl.CostEstimate(flops=2**32, bytes_accessed=2**27, transcendentals=0),
        name="layer",
    )(picks, location, labels, *sends, *constants(groups, tokens, quota))


def onehot(index, count):
    return (jnp.arange(count, dtype=jnp.int32)[:, None] == index[None, :]).astype(BF16)


def shards(query, key, value, labels, partners, out_weight):
    groups = lax.axis_size("clu")
    device = lax.axis_index("clu")
    tokens, features = query.shape
    per_device = tokens // CSIZE
    listed = partners.shape[1]
    quota = (3 * tokens + 2 * groups - 1) // (2 * groups)
    slots = groups * quota
    planes = groups // PLANE
    z, i = device // PLANE, device % PLANE

    wanted = partners.reshape(groups, per_device * listed)
    half = planes // 2
    ahead = jnp.array([0] * planes + [2, 1, -2, -1], jnp.int32)
    distance = jnp.array(list(range(planes)) + [half, half - 1, half, half + 1], jnp.int32)
    there = (z + ahead) % planes
    wanting = there[:, None] * PLANE + (i + jnp.arange(PLANE)) % PLANE
    lists = jnp.take(wanted, wanting, axis=0)
    source = ((there - distance) % planes * PLANE + i)[:, None, None]
    picks = jnp.sum(jnp.where(lists // per_device == source, lists - source * per_device, 0), axis=2)
    my_list = lax.dynamic_slice_in_dim(wanted, device, 1, 0)[0]
    from_group = my_list // per_device
    location = (z - from_group // PLANE) % planes * PLANE + from_group % PLANE

    owner = labels // per_device
    before = jnp.arange(tokens)[None, :] < jnp.arange(tokens)[:, None]
    rank = jnp.sum((owner[:, None] == owner[None, :]) & before, axis=1, dtype=jnp.int32)
    slot = owner * (2 * quota) + rank
    packer = onehot(jnp.concatenate([slot, slot + quota]), 2 * slots)
    cut = GROUPS[0] * HD

    def pack(upper, lower):
        rows = jnp.concatenate([upper, lower], axis=0)
        return exact(packer, rows).astype(BF16).reshape(groups, 2 * quota, rows.shape[1])

    sends = (
        pack(key[:, :cut], value[:, :cut]),
        pack(key[:, cut:], value[:, cut:]),
        pack(query[:, : features // 2], query[:, features // 2 :]),
    )
    returned = layer(
        picks.reshape(-1).astype(jnp.int32),
        location.astype(jnp.int32),
        labels.reshape(1, tokens),
        sends,
        groups,
        per_device,
        listed,
    )
    landed = jnp.concatenate([part.reshape(2 * slots, part.shape[2]) for part in returned], axis=1)
    token_rows = exact(packer.T, landed).astype(BF16)
    lower_cut = cut // 2
    token_rows = jnp.concatenate(
        [
            token_rows[:tokens, :lower_cut],
            token_rows[tokens:, :lower_cut],
            token_rows[:tokens, lower_cut:],
            token_rows[tokens:, lower_cut:],
        ],
        axis=1,
    )
    weight = lax.all_gather(out_weight, "clu", axis=1, tiled=True)
    return project(token_rows, weight, weight.shape[1] // lax.axis_size("head"))


def solution(mesh):
    return jax.shard_map(
        shards,
        mesh=mesh,
        in_specs=(
            P("clu", "head"),
            P("clu", "head"),
            P("clu", "head"),
            P("clu"),
            P(),
            P("head", "clu"),
        ),
        out_specs=P("clu", "head"),
        check_vma=False,
    )
```

time: 676 us -> 404 us (0.60); the launches traced: 667 us -> 404 us
  waiting for transfers between devices: 426 us -> 0.73 us
  Pallas kernels: 0 us -> 366 us
  local copies, waits for them, and re-layouts: 146 us -> 14.3 us
  starting transfers between devices: 62 us -> 0.01 us
    all_to_all x4 -> x0, waiting for transfers between devices: 395 us -> none  [the longest x1 265 us: shards(): lax.all_to_all(cluster_blocks[pick], 'clu', split_axis=0, concat_axis=0,...]
    pallas_call x0 -> x2, Pallas kernels: none -> 366 us  [the longest x1 345 us: layer(): pl.pallas_call(functools.partial(layer_kernel, planes, listed), out_shape...]
    scatter x4 -> x0, local copies, waits for them, and re-layouts: 72.1 us -> none  [the longest x1 37.5 us: shards(): jnp.zeros((groups * token_slots,) + rows.shape[1:], rows.dtype).at[slot]]
    all_to_all x4 -> x0, starting transfers between devices: 61.7 us -> none  [the longest x1 20.6 us: shards(): lax.all_to_all(tags, 'clu', split_axis=0, concat_axis=0, tiled=True)]
    reduce_scatter x1 -> x0, waiting for transfers between devices: 30.7 us -> none  [shards(): lax.psum_scatter(partial_value.astype(jnp.bfloat16), 'head', scatter_dime...]
    gather x7 -> x1, local copies, waits for them, and re-layouts: 29.4 us -> 0.67 us  [shards(): lists = jnp.take(wanted, wanting, axis=0)]
    concatenate x7 -> x0, local copies, waits for them, and re-layouts: 9.44 us -> none  [the longest x3 5.48 us: shards(): jnp.concatenate([cluster_blocks[:, :, 0], listed_blocks[:, :, 0]], axis=1)]
    slice x3 -> x11, local copies, waits for them, and re-layouts: 8.15 us -> 0.11 us  [the longest x1 0.05 us: shards(): query[:, :features // 2]]
  transfers between devices with their start and end apart: 6 -> 1, of which waited for: 4 -> 0; matrix products, arithmetic and copies ran while one was open for 21% -> 3% of each run, Pallas kernels for 0% -> 85%
where the time goes in v3:
time: 404 us
  Pallas kernels  366 us (91%)
  local copies, waits for them, and re-layouts  14.3 us (4%)
  between operations  13.6 us (3%)
  matrix products  7.22 us (2%)
    pallas_call x1, Pallas kernels, layer(): pl.pallas_call(functools.partial(layer_kernel, planes, listed), out_shape...  345 us
    pallas_call x1, Pallas kernels, project(): pl.pallas_call(project_kernel, out_shape=jax.ShapeDtypeStruct((tokens, wi...  20.5 us
  transfers between devices with their start and end apart: 1, of which 0 were waited for; matrix products, arithmetic and copies ran while one was open for 3% of the time, Pallas kernels for 85%

profile of v3, /device:TPU:1, one launch (start us, length us, event | category | flops | bytes accessed | tf_op | source)
XLA Modules:
  0.0 403.9 jit_solution(14931997281455452266)
XLA Ops:
  6.5 0.0 all-gather.2.cloned.1.call-start
  6.5 0.7 all-gather.2.cloned.1.call-update
  7.3 0.0 copy-start.2
  7.3 0.0 slice-start
  7.3 0.0 slice-start.2
  7.3 1.3 reshape.129.refs_2_
  8.6 0.7 broadcast_multiply_fusion
  9.3 0.1 compare_select_fusion
  9.4 0.1 reshape.137
  9.5 0.0 copy-start.1
  9.5 1.3 copy.21
  10.8 0.4 reshape.127
  11.2 0.7 gather_fusion
  11.8 0.1 fusion.32
  11.9 0.5 select_reduce_fusion
  12.4 0.6 reshape.128.refs_0_
  13.1 0.6 fusion.34.refs_1_
  13.7 0.0 copy-done.2
  13.7 0.2 convert_reduce_fusion
  13.9 0.1 pad_add_fusion
  14.0 0.0 slice-done
  14.0 0.0 slice-done.2
  14.0 0.0 slice-start.1
  14.0 0.0 slice-start.3
  14.0 1.4 fusion.14.refs_4_
  15.4 0.0 copy-done.1
  15.4 0.1 fusion.49
  15.5 1.8 fusion.11.refs_5_
  17.3 0.0 slice-done.1
  17.3 0.0 slice-done.3
  17.3 2.0 fusion.6.refs_3_
  19.3 345.2 %layer.1 = (bf16[128,8,256]{2,1,0:T(8,128)(2,1)}, bf16[128,8,128]{2,1,0:T(8,128)(2,1)}) custom-call(s32[160]{0:T(256)} %reshape.128.refs_0_, s32[60]{0:T(128)} %fusion.34.refs_1_, s32[1,320]{1,0:T(1,128)} %reshape.129.refs_2_, bf16[128,8,512]{2,1,0:T(8,128)(2,1)} %fusion.6.refs_3_, bf16[128,8,256]{2,1,0:T(8,128)(2,1)} %fusion.14.refs_4_, ...), custom_call_target="tpu_custom_call" | custom-call | flops 4294967296 | bytes 134217728 | tf_op jit(solution)/shard_map/layer/pallas_call | solution.py:483
  364.5 2.0 fusion.13
  366.7 0.0 all-gather.2.cloned.1.call-done
  366.7 6.7 %copy.22.weight_ref = bf16[768,3072]{1,0:T(8,128)(2,1)} copy(bf16[768,3072]{0,1:T(8,128)(2,1)} %all-gather.2.cloned.1.call-done) | data formatting | bytes 9437184 | tf_op jit(solution)/shard_map/all_gather | solution.py:573
  373.4 0.0 copy-start
  373.4 2.3 copy-done
  375.8 20.5 %project.1 = bf16[320,768]{1,0:T(8,128)(2,1)S(1)} custom-call(bf16[320,768]{1,0:T(8,128)(2,1)S(1)} %pad_maximum_fusion.rows_ref, bf16[768,3072]{1,0:T(8,128)(2,1)S(1)} %copy-done), custom_call_target="tpu_custom_call" | custom-call | flops 2147483648 | bytes 8388608 | tf_op jit(solution)/shard_map/project/pallas_call | solution.py:422
  396.3 0.8 copy.24
  (8 shorter events, 0.1 us)
Async XLA Ops:
  6.5 360.2 %all-gather.2.cloned.1.call-start = ((), (), s32[]{:S(2)}) async-start(), calls=%async_computation | async-start | bytes 4755456 | tf_op jit(solution)/shard_map/all_gather | solution.py:573
  7.3 6.4 %copy-start.2 = (s32[320]{0:T(512)S(1)}, s32[320]{0:T(512)}, u32[]{:S(2)}) copy-start(s32[320]{0:T(512)} %param.17) | copy-start | bytes 3844
  7.3 6.7 %slice-start = ((bf16[320,768]{1,0:T(8,128)(2,1)}), bf16[320,256]{1,0:T(8,128)(2,1)S(1)}, s32[]{:S(2)}) async-start(bf16[320,768]{1,0:T(8,128)(2,1)} %param.15), calls=%async_computation.1 | async-start | bytes 327680 | tf_op jit(solution)/shard_map/slice | solution.py:549
  7.3 6.7 %slice-start.2 = ((bf16[320,768]{1,0:T(8,128)(2,1)}), bf16[320,256]{1,0:T(8,128)(2,1)S(1)}, s32[]{:S(2)}) async-start(bf16[320,768]{1,0:T(8,128)(2,1)} %param.16), calls=%async_computation.3 | async-start | bytes 327680 | tf_op jit(solution)/shard_map/slice | solution.py:549
  9.5 6.0 %copy-start.1 = (bf16[320,768]{1,0:T(8,128)(2,1)S(1)}, bf16[320,768]{1,0:T(8,128)(2,1)}, u32[]{:S(2)}) copy-start(bf16[320,768]{1,0:T(8,128)(2,1)} %param.14) | copy-start | bytes 1474564
  14.0 3.3 slice-start.1
  14.0 3.3 slice-start.3
  373.4 2.3 copy-start
Sparse Core Ops, SparseCore 0:
  10.4 171.7 all-gather.1

commit v4 on v3

--- a/solution.py
+++ b/solution.py
@@ -35,8 +35,8 @@
     def __init__(self, planes, z, i, pick, kv, out, ups, downs, packs, near, far, stage, sems):
         self.planes, self.half, self.full = planes, planes // 2, planes // 2 - 2
         self.z, self.i = z, i
-        self.above = lax.rem(z + 1, planes) * PLANE + i
-        self.below = lax.rem(z + planes - 1, planes) * PLANE + i
+        self.above = lax.rem(z + 1, planes)
+        self.below = lax.rem(z + planes - 1, planes)
         self.pick, self.kv, self.out = pick, kv, out
         self.ups, self.downs = (kv,) + ups, (kv,) + downs
         self.packs, self.near, self.far, self.stage = packs, near, far, stage
@@ -50,7 +50,7 @@
             dst_ref=dst,
             send_sem=send,
             recv_sem=recv,
-            device_id={"clu": self.above if up else self.below},
+            device_id={"z": self.above if up else self.below},
             device_id_type=MESH,
         )
 
@@ -81,7 +81,7 @@
             dst_ref=self.out.at[k * PLANE + self.i],
             send_sem=self.side_send,
             recv_sem=self.side_recv,
-            device_id={"clu": self.z * PLANE + lax.rem(self.i + j, PLANE)},
+            device_id={"plane": lax.rem(self.i + j, PLANE)},
             device_id_type=MESH,
         )
 
@@ -185,12 +185,13 @@
 
 
 def layer_kernel(planes, listed, *refs):
-    (pick, loc, labels_ref, send0, send1, sendq, upto, lower, col, row, col_mask, row_mask, ret0, ret1, *rest) = refs
-    (arr0, arr1, arrq, all_ref, lab, dcol, drow, q_ref, back0, back1, o0, o1, *rest) = rest
+    (pick, loc, labels_ref, slot_row, slot_col, query, key, value, *rest) = refs
+    (upto, lower, col, row, col_mask, row_mask, rows_out, *rest) = rest
+    (send0, send1, sendq, ret0, ret1, packc, packr, arr0, arr1, arrq, all_ref, lab, dcol, drow, q_ref, back0, back1, o0, o1, *rest) = rest
     (a2a_send, a2a_recv, tag_send, tag_recv, tag_side_send, tag_side_recv, *rest) = rest
     per_ring = len(rest) // 2
-    me = lax.axis_index("clu")
-    z, i = me // PLANE, me % PLANE
+    z, i = lax.axis_index("z"), lax.axis_index("plane")
+    me = z * PLANE + i
     half, full, total = planes // 2, planes // 2 - 2, planes * PLANE
     hops = [half]
     for d in range(half - 1, 0, -1):
@@ -203,16 +204,33 @@
         rings.append(Ring(planes, z, i, pick, kv, out, ups, downs, *more[:4], more[4:]))
 
     def at(dz, j):
-        return lax.rem(z + dz + planes, planes) * PLANE + lax.rem(i + j, PLANE)
+        return lax.rem(z + dz + planes, planes), lax.rem(i + j, PLANE)
 
     barrier = pltpu.get_barrier_semaphore()
 
     def greet(r, carry):
         other = lax.rem(me + r, total)
-        pl.semaphore_signal(barrier, inc=1, device_id={"clu": other}, device_id_type=MESH)
+        there = {"z": other // PLANE, "plane": other % PLANE}
+        pl.semaphore_signal(barrier, inc=1, device_id=there, device_id_type=MESH)
         return carry
 
     lax.fori_loop(1, total, greet, 0)
+
+    def to_blocks(hots, upper, lower, block):
+        for l in range(0, block.shape[2], LANES):
+            part = exact(hots[0], upper(l)) + exact(hots[1], lower(l))
+            block[:, :, l : l + LANES] = part.reshape(total, block.shape[1], LANES).astype(BF16)
+
+    def columns(ref, first):
+        return lambda l: ref[:, first + l : first + l + LANES]
+
+    slots, tokens = packc.shape[1], packc.shape[2]
+    cut = GROUPS[0] * HD
+    quota = send0.shape[1] // 2
+    for p in range(2):
+        number = lax.broadcasted_iota(jnp.int32, (slots, tokens), 0).astype(F32)
+        packc[p] = jnp.where(number == slot_row[...] + float(p * quota), 1.0, 0.0).astype(BF16)
+    to_blocks(packc, columns(key, 0), columns(value, 0), send0)
     pl.semaphore_wait(barrier, total - 1)
 
     def tag(dz, source):
@@ -221,7 +239,7 @@
             dst_ref=all_ref.at[i, source],
             send_sem=tag_send.at[dz % planes],
             recv_sem=tag_recv.at[source],
-            device_id={"clu": at(dz, 0)},
+            device_id={"z": at(dz, 0)[0]},
             device_id_type=MESH,
         )
 
@@ -231,18 +249,18 @@
             dst_ref=all_ref.at[source],
             send_sem=tag_side_send.at[j],
             recv_sem=tag_side_recv.at[source],
-            device_id={"clu": at(0, j)},
+            device_id={"plane": at(0, j)[1]},
             device_id_type=MESH,
         )
 
     def exchange(n, block, landed):
         def start(to):
             pltpu.make_async_remote_copy(
-                src_ref=block.at[to],
+                src_ref=block.at[to[0] * PLANE + to[1]],
                 dst_ref=landed.at[me],
                 send_sem=a2a_send.at[n],
                 recv_sem=a2a_recv.at[n],
-                device_id={"clu": to},
+                device_id={"z": to[0], "plane": to[1]},
                 device_id_type=MESH,
             ).start()
 
@@ -270,8 +288,13 @@
         tag(dz, lax.rem(z - dz + planes, planes)).wait_recv()
     for j in range(1, PLANE):
         tag_side(j, i).start()
+    to_blocks(packc, columns(key, cut), columns(value, cut), send1)
     exchange(1, send1, arr1)
+    to_blocks(packc, columns(query, 0), columns(query, query.shape[1] // 2), sendq)
     exchange(2, sendq, arrq)
+    for p in range(2):
+        number = lax.broadcasted_iota(jnp.int32, (tokens, slots), 1).astype(F32)
+        packr[p] = jnp.where(number == slot_col[...] + float(p * quota), 1.0, 0.0).astype(BF16)
     for j in range(1, PLANE):
         tag_side(j, lax.rem(i - j + PLANE, PLANE)).wait_recv()
 
@@ -279,7 +302,6 @@
         for ii in range(PLANE):
             lab[zz * PLANE + ii : zz * PLANE + ii + 1, :] = all_ref[ii, zz]
     per_device = q_ref.shape[0]
-    quota = send0.shape[1] // 2
     local = lab[...] - me * per_device
     mine = jnp.logical_and(local >= 0, local < per_device)
     order = exact(jnp.where(mine, 1.0, 0.0).astype(BF16), upto[...])
@@ -300,7 +322,6 @@
         earlier = earlier + marks[r]
     wide = exact(col[...], table.astype(BF16))
     tall = exact(table.T.astype(BF16), row[...])
-    slots, tokens = dcol.shape[1], dcol.shape[2]
     for p in range(2):
         to = jnp.sum(wide * col_mask[p], axis=1, keepdims=True)
         rows = lax.broadcasted_iota(jnp.int32, (slots, tokens), 1).astype(F32)
@@ -309,20 +330,29 @@
         rows = lax.broadcasted_iota(jnp.int32, (tokens, slots), 0).astype(F32)
         drow[p] = jnp.where(rows == to, 1.0, 0.0).astype(BF16)
 
-    def unpack(landed, target):
+    def from_blocks(hots, landed, store):
         width = landed.shape[2]
         for l in range(0, width, LANES):
             block = landed[:, :, l : l + LANES].astype(F32).reshape(slots, LANES).astype(BF16)
             for p in range(2):
-                part = exact(drow[p], block).astype(BF16).reshape(per_device, CSIZE, LANES)
-                target[:, :, p * width + l : p * width + l + LANES] = part
+                store(p * width + l, exact(hots[p], block).astype(BF16))
+
+    def unpack(landed, target):
+        def store(at, part):
+            target[:, :, at : at + LANES] = part.reshape(per_device, CSIZE, LANES)
+
+        from_blocks(drow, landed, store)
 
     def give_back(n, attended, back, ret):
-        width = back.shape[2]
-        for l in range(0, width, LANES):
-            part = exact(dcol[0], attended[:, l : l + LANES]) + exact(dcol[1], attended[:, width + l : width + l + LANES])
-            back[:, :, l : l + LANES] = part.reshape(total, 2 * quota, LANES).astype(BF16)
+        to_blocks(dcol, columns(attended, 0), columns(attended, back.shape[2]), back)
         exchange(n, back, ret)
+
+    def receive_back(n, ret, first):
+        def store(at, part):
+            rows_out[:, first + at : first + at + LANES] = part
+
+        landed_all(n, ret)
+        from_blocks(packr, ret, store)
 
     first, second = rings
     landed_all(0, arr0)
@@ -344,6 +374,7 @@
     for d in range(3, full + 1):
         second.advance(d)
     second.last_hops()
+    receive_back(3, ret0, 0)
     second.arrive()
     attend(listed, GROUPS[0], GROUPS[1], loc, q_ref, second.kv, second.out, o1)
     give_back(4, o1, back1, ret1)
@@ -356,24 +387,38 @@
     second.finish()
     for n, block in enumerate((send0, send1, sendq, back0, back1)):
         drain(block, total - 1, a2a_send.at[n])
-    landed_all(3, ret0)
-    landed_all(4, ret1)
-
-
-def project_kernel(rows_ref, weight_ref, out_ref, sent, came, near, send, recv):
+    receive_back(4, ret1, cut)
+
+
+def project_kernel(planes, rows_ref, weight_ref, order_ref, out_ref, held, sent, came, near, load, send, recv):
     n = lax.axis_size("head")
     x = lax.axis_index("head")
-    left, right = lax.rem(x + n - 1, n), lax.rem(x + 1, n)
+    left, right, opposite = lax.rem(x + n - 1, n), lax.rem(x + 1, n), lax.rem(x + 2, n)
     width = out_ref.shape[1]
     part = width // 2
-
-    def block(to, first, count):
-        start = pl.multiple_of(to * width + first, LANES)
-        return exact(rows_ref[...], weight_ref[:, pl.ds(start, count)])
+    piece = width // PLANE
+    owners = (opposite, right, left, x)
+    for at, to in enumerate(owners):
+        for p in range(PLANE):
+            source = pl.multiple_of(p * (n * piece) + to * piece, piece)
+            pltpu.make_async_copy(
+                weight_ref.at[pl.ds(source, piece)], held.at[at, pl.ds(p * piece, piece)], load.at[at]
+            ).start()
 
     barrier = pltpu.get_barrier_semaphore()
     for other in (left, right):
         pl.semaphore_signal(barrier, inc=1, device_id={"head": other}, device_id_type=MESH)
+
+    def block(at, half):
+        return lax.dot_general(
+            rows_ref[...],
+            held[at, half * part : (half + 1) * part],
+            (((1,), (1,)), ((), ())),
+            preferred_element_type=F32,
+        )
+
+    def ready(at):
+        pltpu.make_async_copy(held.at[at], held.at[at], load.at[at]).wait()
 
     def copy(way, piece, src, dst):
         return pltpu.make_async_remote_copy(
@@ -385,58 +430,75 @@
             device_id_type=MESH,
         )
 
-    copies = [[copy(w, 0, sent.at[w, 0], near.at[w])] + [copy(w, p, sent.at[w, p], came.at[w, p - 1]) for p in (1, 2)] for w in range(2)]
-    opposite = lax.rem(x + 2, n)
-    for w in range(2):
-        sent[w, 0] = block(opposite, w * part, part).astype(BF16)
+    copies = []
+    for w in range(2):
+        copies.append([copy(w, 0, sent.at[w, 0], near.at[w])])
+        copies[w] += [copy(w, p, sent.at[w, p], came.at[w, p - 1]) for p in (1, 2)]
+    ready(0)
+    for w in range(2):
+        sent[w, 0] = block(0, w).astype(BF16)
     pl.semaphore_wait(barrier, 2)
     for w in range(2):
         copies[w][0].start()
     for w in range(2):
-        sent[w, 1] = block(right if w == 0 else left, (1 - w) * part, part).astype(BF16)
+        ready(1 + w)
+        sent[w, 1] = block(1 + w, 1 - w).astype(BF16)
         copies[w][1].start()
-    summed = [block(right if w == 0 else left, w * part, part) for w in range(2)]
+    summed = [block(1 + w, w) for w in range(2)]
     for w in range(2):
         copies[w][0].wait_recv()
         sent[w, 2] = (summed[w].astype(BF16).astype(F32) + near[w].astype(F32)).astype(BF16)
         copies[w][2].start()
-    own = [block(x, h * part, part).astype(BF16).astype(F32) for h in range(2)]
+    ready(3)
+    own = [block(3, h).astype(BF16).astype(F32) for h in range(2)]
     for w in range(2):
         copies[w][1].wait_recv()
     for w in range(2):
         copies[w][2].wait_recv()
+    result = jnp.zeros(out_ref.shape, F32)
     for h in range(2):
         total = own[h]
         for w in range(2):
             total = total + came[w, 1 if h == w else 0].astype(F32)
-        out_ref[:, h * part : (h + 1) * part] = total.astype(BF16)
+        result = result + exact(total.astype(BF16), order_ref[h * part : (h + 1) * part])
+    out_ref[...] = result.astype(BF16)
     for w in range(2):
         for p in range(3):
             copies[w][p].wait_send()
 
 
-def project(rows, weight, width):
-    tokens = rows.shape[0]
+def project(rows, weight, planes):
+    tokens, features = rows.shape
+    heads = lax.axis_size("head")
+    width = weight.shape[0] // heads
     half = (tokens, width // 2)
+    each = width // PLANE // (planes // heads)
+    order = np.zeros((width, width), np.float32)
+    for p in range(PLANE):
+        for zz in range(planes // heads):
+            for c in range(each):
+                order[(p * (planes // heads) + zz) * each + c, (zz * PLANE + p) * each + c] = 1.0
     dma = pltpu.SemaphoreType.DMA
     return pl.pallas_call(
-        project_kernel,
+        functools.partial(project_kernel, planes),
         out_shape=jax.ShapeDtypeStruct((tokens, width), BF16),
-        in_specs=[VMEM, VMEM],
+        in_specs=[VMEM, pl.BlockSpec(memory_space=pl.ANY), VMEM],
         out_specs=VMEM,
         scratch_shapes=[
+            pltpu.VMEM((heads, width, features), BF16),
             pltpu.VMEM((2, 3) + half, BF16),
             pltpu.VMEM((2, 2) + half, BF16),
             pltpu.VMEM((2,) + half, BF16),
+            dma((heads,)),
             dma((2, 3)),
             dma((2, 3)),
         ],
         compiler_params=pltpu.CompilerParams(
-            collective_id=1, has_side_effects=True, vmem_limit_bytes=24 * 2**20
+            collective_id=1, has_side_effects=True, vmem_limit_bytes=60 * 2**20
         ),
         cost_estimate=pl.CostEstimate(flops=2**31, bytes_accessed=2**23, transcendentals=0),
         name="project",
-    )(rows, weight)
+    )(rows, weight, jnp.asarray(order, BF16))
 
 
 def constants(groups, tokens, quota):
@@ -458,11 +520,11 @@
     return as16(upto), as16(lower), as16(col), as16(col.T), jnp.asarray(col_mask), jnp.asarray(row_mask)
 
 
-def layer(picks, location, labels, sends, groups, per_device, listed):
+def layer(picks, location, labels, slot, query, key, value, groups, quota, listed):
     planes = groups // PLANE
     full = planes // 2 - 2
-    tokens = per_device * CSIZE
-    quota = sends[0].shape[1] // 2
+    tokens, features = query.shape
+    per_device = tokens // CSIZE
     slots = 2 * groups * quota
     dma = pltpu.SemaphoreType.DMA
 
@@ -470,8 +532,9 @@
         return pltpu.VMEM(shape, BF16)
 
     widths = [heads * HD for heads in GROUPS]
-    landings = [scratch(*x.shape) for x in sends]
+    sends = [scratch(groups, 2 * quota, w) for w in widths + [features // 2]]
     backs = [(groups, 2 * quota, w // 2) for w in widths]
+    hots = [scratch(2, slots, tokens), scratch(2, tokens, slots)]
     rings = []
     for w in widths:
         shard, block = (per_device, CSIZE, 2 * w), (CSIZE, 2 * w)
@@ -482,15 +545,17 @@
         rings += [dma((2, full, SUBS)), dma((2, full, SUBS)), dma((2, 3)), dma((2, 3)), dma, dma]
     return pl.pallas_call(
         functools.partial(layer_kernel, planes, listed),
-        out_shape=tuple(jax.ShapeDtypeStruct(b, BF16) for b in backs),
-        in_specs=[SMEM, SMEM] + [VMEM] * 10,
-        out_specs=(VMEM, VMEM),
-        scratch_shapes=landings
+        out_shape=jax.ShapeDtypeStruct((tokens, features), BF16),
+        in_specs=[SMEM, SMEM] + [VMEM] * 12,
+        out_specs=VMEM,
+        scratch_shapes=sends
+        + [scratch(*b) for b in backs]
+        + hots
+        + sends
         + [
-            pltpu.VMEM((PLANE, planes) + labels.shape, labels.dtype),
+            pltpu.VMEM((PLANE, planes, 1, tokens), labels.dtype),
             pltpu.VMEM((groups, tokens), labels.dtype),
-            scratch(2, slots, tokens),
-            scratch(2, tokens, slots),
+            *hots,
             scratch(per_device, CSIZE, sum(widths)),
         ]
         + [scratch(*b) for b in backs]
@@ -502,23 +567,28 @@
         ),
         cost_estimate=pl.CostEstimate(flops=2**32, bytes_accessed=2**27, transcendentals=0),
         name="layer",
-    )(picks, location, labels, *sends, *constants(groups, tokens, quota))
-
-
-def onehot(index, count):
-    return (jnp.arange(count, dtype=jnp.int32)[:, None] == index[None, :]).astype(BF16)
+    )(
+        picks,
+        location,
+        labels.reshape(1, tokens),
+        slot.reshape(1, tokens).astype(F32),
+        slot.reshape(tokens, 1).astype(F32),
+        query,
+        key,
+        value,
+        *constants(groups, tokens, quota),
+    )
 
 
 def shards(query, key, value, labels, partners, out_weight):
-    groups = lax.axis_size("clu")
-    device = lax.axis_index("clu")
+    planes = lax.axis_size("z")
+    groups = planes * PLANE
+    z, i = lax.axis_index("z"), lax.axis_index("plane")
+    device = z * PLANE + i
     tokens, features = query.shape
     per_device = tokens // CSIZE
     listed = partners.shape[1]
     quota = (3 * tokens + 2 * groups - 1) // (2 * groups)
-    slots = groups * quota
-    planes = groups // PLANE
-    z, i = device // PLANE, device % PLANE
 
     wanted = partners.reshape(groups, per_device * listed)
     half = planes // 2
@@ -537,55 +607,38 @@
     before = jnp.arange(tokens)[None, :] < jnp.arange(tokens)[:, None]
     rank = jnp.sum((owner[:, None] == owner[None, :]) & before, axis=1, dtype=jnp.int32)
     slot = owner * (2 * quota) + rank
-    packer = onehot(jnp.concatenate([slot, slot + quota]), 2 * slots)
-    cut = GROUPS[0] * HD
-
-    def pack(upper, lower):
-        rows = jnp.concatenate([upper, lower], axis=0)
-        return exact(packer, rows).astype(BF16).reshape(groups, 2 * quota, rows.shape[1])
-
-    sends = (
-        pack(key[:, :cut], value[:, :cut]),
-        pack(key[:, cut:], value[:, cut:]),
-        pack(query[:, : features // 2], query[:, features // 2 :]),
-    )
-    returned = layer(
+    token_rows = layer(
         picks.reshape(-1).astype(jnp.int32),
         location.astype(jnp.int32),
-        labels.reshape(1, tokens),
-        sends,
+        labels,
+        slot,
+        query,
+        key,
+        value,
         groups,
-        per_device,
+        quota,
         listed,
     )
-    landed = jnp.concatenate([part.reshape(2 * slots, part.shape[2]) for part in returned], axis=1)
-    token_rows = exact(packer.T, landed).astype(BF16)
-    lower_cut = cut // 2
-    token_rows = jnp.concatenate(
-        [
-            token_rows[:tokens, :lower_cut],
-            token_rows[tokens:, :lower_cut],
-            token_rows[:tokens, lower_cut:],
-            token_rows[tokens:, lower_cut:],
-        ],
-        axis=1,
-    )
-    weight = lax.all_gather(out_weight, "clu", axis=1, tiled=True)
-    return project(token_rows, weight, weight.shape[1] // lax.axis_size("head"))
+    weight = lax.all_gather(out_weight.T, "z", axis=0, tiled=True)
+    weight = lax.all_gather(weight, "plane", axis=0, tiled=True)
+    return project(token_rows, weight, planes)
 
 
 def solution(mesh):
+    heads = mesh.shape["head"]
+    mesh = jax.sharding.Mesh(mesh.devices.reshape(-1, PLANE, heads), ("z", "plane", "head"))
+    clu = ("z", "plane")
     return jax.shard_map(
         shards,
         mesh=mesh,
         in_specs=(
-            P("clu", "head"),
-            P("clu", "head"),
-            P("clu", "head"),
-            P("clu"),
+            P(clu, "head"),
+            P(clu, "head"),
+            P(clu, "head"),
+            P(clu),
             P(),
-            P("head", "clu"),
+            P("head", clu),
         ),
-        out_specs=P("clu", "head"),
+        out_specs=P(clu, "head"),
         check_vma=False,
     )

time: 404 us -> 414 us (1.025)
  blocking collectives: 0 us -> 35.4 us
  Pallas kernels: 366 us -> 356 us
  local copies, waits for them, and re-layouts: 14.3 us -> 6.07 us
  matrix products: 7.22 us -> 0 us
    all_gather x0 -> x1, blocking collectives: none -> 35.4 us  [shards(): weight = lax.all_gather(out_weight.T, 'z', axis=0, tiled=True)]
    pallas_call x1, Pallas kernels: 345 us -> 331 us  [layer(): pl.pallas_call(functools.partial(layer_kernel, planes, listed), out_shape...]
    dot_general x4 -> x0, matrix products: 7.22 us -> none  [exact(): return jnp.dot(a, b, preferred_element_type=F32)]
    all_gather x1 -> x0, local copies, waits for them, and re-layouts: 6.74 us -> none  [shards(): weight = lax.all_gather(out_weight, 'clu', axis=1, tiled=True)]
    pallas_call x1, Pallas kernels: 20.5 us -> 24.9 us  [project(): pl.pallas_call(functools.partial(project_kernel, planes), out_shape=jax.S...]
  transfers between devices with their start and end apart: 1 -> 1, of which waited for: 0 -> 0; matrix products, arithmetic and copies ran while one was open for 3% -> 2% of each run, Pallas kernels for 85% -> 80%
where the time goes in v4:
time: 414 us; the launch traced here: 413 us
  Pallas kernels  356 us (86%)
  blocking collectives  35.4 us (9%)
  between operations  13.5 us (3%)
  local copies, waits for them, and re-layouts  6.07 us (1%)
    pallas_call x1, Pallas kernels, layer(): pl.pallas_call(functools.partial(layer_kernel, planes, listed), out_shape...  331 us
    all_gather x1, blocking collectives, shards(): weight = lax.all_gather(out_weight.T, 'z', axis=0, tiled=True)  35.4 us
    pallas_call x1, Pallas kernels, project(): pl.pallas_call(functools.partial(project_kernel, planes), out_shape=jax.S...  24.9 us
  transfers between devices with their start and end apart: 1, of which 0 were waited for; matrix products, arithmetic and copies ran while one was open for 2% of the time, Pallas kernels for 80%

profile of v4, /device:TPU:1, one launch (start us, length us, event | category | flops | bytes accessed | tf_op | source)
XLA Modules:
  0.0 413.5 jit_solution(3363998740710662242)
XLA Ops:
  6.5 0.0 copy-start.2
  6.5 0.0 copy-start.3
  6.5 0.0 copy-start.1
  6.5 0.0 copy-start
  6.5 0.0 all-gather.2.cloned.1.call-start
  6.6 35.4 %all_gather.6 = bf16[384,768]{1,0:T(8,128)(2,1)} all-gather(bf16[24,768]{1,0:T(8,128)(2,1)} %bitcast.15), channel_id=1, replica_groups=mesh['z'=16,'plane'=8,'head'=4] {'z'}, dimensions={0}, use_global_device_ids=true | all-gather | bytes 626688 | tf_op jit(solution)/shard_map/all_gather | solution.py:622
  42.0 0.0 all-gather.2.cloned.1.call-update
  42.0 0.7 add_select_fusion.1
  42.7 0.2 convert_reduce_fusion
  42.9 0.7 add_convert_fusion
  43.7 0.8 convert_element_type.15.refs_4_
  44.4 0.6 convert_element_type.13.refs_3_
  45.0 0.0 copy-done.1
  45.0 0.6 reshape.117.refs_2_
  45.6 0.0 copy-done.2
  45.6 0.0 copy-done.3
  45.7 0.1 compare_select_fusion
  45.7 0.1 reshape.120
  45.8 0.0 copy-done
  45.8 0.4 copy.19
  46.3 0.4 reshape.115
  46.7 0.7 gather_fusion
  47.4 0.1 fusion.5
  47.4 0.5 select_reduce_fusion
  47.9 0.7 reshape.116.refs_0_
  48.6 0.6 fusion.7.refs_1_
  49.2 330.6 %layer.1.rows_ref = bf16[320,768]{1,0:T(8,128)(2,1)} custom-call(s32[160]{0:T(256)} %reshape.116.refs_0_, s32[60]{0:T(128)} %fusion.7.refs_1_, s32[1,320]{1,0:T(1,128)} %reshape.117.refs_2_, f32[1,320]{1,0:T(1,128)} %convert_element_type.13.refs_3_, f32[320,1]{1,0:T(8,128)} %convert_element_type.15.refs_4_, bf16[320,768]{1,0:T(8,128)(2,1)} %refs_5_.1, ...), custom_call_target="tpu_custom_call" | custom-call | flops 4294967296 | bytes 134217728 | tf_op jit(solution)/shard_map/layer/pallas_call | solution.py:546
  379.9 0.0 all-gather.2.cloned.1.call-done.weight_ref
  379.9 24.9 %project.1 = bf16[320,768]{1,0:T(8,128)(2,1)} custom-call(bf16[320,768]{1,0:T(8,128)(2,1)} %layer.1.rows_ref, bf16[3072,768]{1,0:T(8,128)(2,1)} %all-gather.2.cloned.1.call-done.weight_ref, bf16[768,768]{1,0:T(8,128)(2,1)} %constant.136.clone.order_ref), custom_call_target="tpu_custom_call" | custom-call | flops 2147483648 | bytes 8388608 | tf_op jit(solution)/shard_map/project/pallas_call | solution.py:482
  404.8 1.8 copy.22
  (4 shorter events, 0.0 us)
Async XLA Ops:
  6.5 39.1 %copy-start.2 = (s32[20]{0:T(128)S(1)}, s32[20]{0:T(128)}, u32[]{:S(2)}) copy-start(s32[20]{0:T(128)} %constant.128.clone) | copy-start | bytes 244
  6.5 39.1 %copy-start.3 = (s32[20]{0:T(128)S(1)}, s32[20]{0:T(128)}, u32[]{:S(2)}) copy-start(s32[20]{0:T(128)} %constant.142) | copy-start | bytes 244
  6.5 38.5 %copy-start.1 = (s32[320]{0:T(512)S(1)}, s32[320]{0:T(512)}, u32[]{:S(2)}) copy-start(s32[320]{0:T(512)} %param.18) | copy-start | bytes 3844
  6.5 39.3 %copy-start = (s32[2560,3]{0,1:T(4,128)S(1)}, s32[2560,3]{0,1:T(4,128)}, u32[]{:S(2)}) copy-start(s32[2560,3]{0,1:T(4,128)} %param.19) | copy-start | bytes 92164
  6.5 373.4 %all-gather.2.cloned.1.call-start = ((), (), s32[]{:S(2)}) async-start(), calls=%async_computation | async-start | bytes 5308416 | tf_op jit(solution)/shard_map/all_gather | solution.py:623
Sparse Core Ops, SparseCore 0:
  42.1 55.2 all-gather.1

commit v5 on v4

--- a/solution.py
+++ b/solution.py
@@ -184,13 +184,15 @@
     lax.fori_loop(0, q_ref.shape[0] // 2, body, 0)
 
 
-def layer_kernel(planes, listed, *refs):
-    (pick, loc, labels_ref, slot_row, slot_col, query, key, value, *rest) = refs
-    (upto, lower, col, row, col_mask, row_mask, rows_out, *rest) = rest
+def layer_kernel(planes, heads, listed, *refs):
+    (pick, loc, labels_ref, slot_row, slot_col, query, key, value, weight, *rest) = refs
+    (upto, lower, col, row, col_mask, row_mask, ordered, out_ref, *rest) = rest
     (send0, send1, sendq, ret0, ret1, packc, packr, arr0, arr1, arrq, all_ref, lab, dcol, drow, q_ref, back0, back1, o0, o1, *rest) = rest
+    (w_ring, w_all, rows0, rows1, total0, w_send, w_recv, w_head, w_side, t_send, t_recv, *rest) = rest
     (a2a_send, a2a_recv, tag_send, tag_recv, tag_side_send, tag_side_recv, *rest) = rest
     per_ring = len(rest) // 2
     z, i = lax.axis_index("z"), lax.axis_index("plane")
+    x = lax.axis_index("head")
     me = z * PLANE + i
     half, full, total = planes // 2, planes // 2 - 2, planes * PLANE
     hops = [half]
@@ -215,6 +217,9 @@
         return carry
 
     lax.fori_loop(1, total, greet, 0)
+    for dx in range(1, heads):
+        pl.semaphore_signal(barrier, inc=1, device_id={"head": lax.rem(x + dx, heads)}, device_id_type=MESH)
+    meetings = total + heads - 2
 
     def to_blocks(hots, upper, lower, block):
         for l in range(0, block.shape[2], LANES):
@@ -231,7 +236,7 @@
         number = lax.broadcasted_iota(jnp.int32, (slots, tokens), 0).astype(F32)
         packc[p] = jnp.where(number == slot_row[...] + float(p * quota), 1.0, 0.0).astype(BF16)
     to_blocks(packc, columns(key, 0), columns(value, 0), send0)
-    pl.semaphore_wait(barrier, total - 1)
+    pl.semaphore_wait(barrier, meetings)
 
     def tag(dz, source):
         return pltpu.make_async_remote_copy(
@@ -280,17 +285,91 @@
     def landed_all(n, landed):
         drain(landed, total - 1, a2a_recv.at[n])
 
+    def plane_at(d, up):
+        return lax.rem(z + planes - d, planes) if up else lax.rem(z + d, planes)
+
+    def weight_hop(d, up, block):
+        n = 0 if up else 1
+        return pltpu.make_async_remote_copy(
+            src_ref=w_ring.at[block],
+            dst_ref=w_ring.at[block],
+            send_sem=w_send.at[n, d - 1],
+            recv_sem=w_recv.at[n, d - 1],
+            device_id={"z": plane_at(1, not up)},
+            device_id_type=MESH,
+        )
+
+    def weight_begins():
+        w_ring[z] = weight[...]
+        for up in (True, False):
+            weight_hop(1, up, z).start()
+
+    def weight_goes_on(d):
+        for up in (True, False):
+            if d < half or up:
+                weight_hop(d, up, plane_at(d, up)).wait_recv()
+                if d + 1 < half or (d + 1 == half and up):
+                    weight_hop(d + 1, up, plane_at(d, up)).start()
+
+    zs = planes // heads
+
+    def weight_head(to, source):
+        return pltpu.make_async_remote_copy(
+            src_ref=w_ring.at[pl.ds(to * zs, zs)],
+            dst_ref=w_all.at[i, source],
+            send_sem=w_head.at[0, to],
+            recv_sem=w_head.at[1, source],
+            device_id={"head": to},
+            device_id_type=MESH,
+        )
+
+    def weight_side(j, source):
+        return pltpu.make_async_remote_copy(
+            src_ref=w_all.at[i],
+            dst_ref=w_all.at[source],
+            send_sem=w_side.at[0, j],
+            recv_sem=w_side.at[1, source],
+            device_id={"plane": lax.rem(i + j, PLANE)},
+            device_id_type=MESH,
+        )
+
+    def rows_head(g, dx, source):
+        rows = (rows0, rows1)[g]
+        return pltpu.make_async_remote_copy(
+            src_ref=rows.at[x],
+            dst_ref=rows.at[source],
+            send_sem=t_send.at[g, dx],
+            recv_sem=t_recv.at[g, source],
+            device_id={"head": lax.rem(x + dx, heads)},
+            device_id_type=MESH,
+        )
+
+    def products(rows, first, part):
+        width = rows.shape[2]
+        held = PLANE // 2
+        result = 0.0
+        for xx in range(heads):
+            block = w_all[part * held : (part + 1) * held, xx, :, :, first : first + width].astype(F32)
+            block = block.reshape(block.shape[0] * block.shape[1] * block.shape[2], width).astype(BF16)
+            result = result + lax.dot_general(
+                rows[xx], block, (((1,), (1,)), ((), ())), preferred_element_type=F32
+            )
+        return result
+
     for dz in hops:
         tag(dz, z).start()
     all_ref[i, z] = labels_ref[...]
+    weight_begins()
     exchange(0, send0, arr0)
     for dz in hops:
         tag(dz, lax.rem(z - dz + planes, planes)).wait_recv()
     for j in range(1, PLANE):
         tag_side(j, i).start()
     to_blocks(packc, columns(key, cut), columns(value, cut), send1)
+    weight_goes_on(1)
     exchange(1, send1, arr1)
     to_blocks(packc, columns(query, 0), columns(query, query.shape[1] // 2), sendq)
+    weight_goes_on(2)
     exchange(2, sendq, arrq)
     for p in range(2):
         number = lax.broadcasted_iota(jnp.int32, (tokens, slots), 1).astype(F32)
@@ -347,19 +426,38 @@
         to_blocks(dcol, columns(attended, 0), columns(attended, back.shape[2]), back)
         exchange(n, back, ret)
 
-    def receive_back(n, ret, first):
+    def receive_back(n, ret, g):
+        rows = (rows0, rows1)[g]
+
         def store(at, part):
-            rows_out[:, first + at : first + at + LANES] = part
+            rows[x, :, at : at + LANES] = part
 
         landed_all(n, ret)
         from_blocks(packr, ret, store)
+        for dx in range(1, heads):
+            rows_head(g, dx, x).start()
+
+    def rows_gathered(g):
+        for dx in range(1, heads):
+            rows_head(g, dx, lax.rem(x + heads - dx, heads)).wait_recv()
 
     first, second = rings
     landed_all(0, arr0)
     unpack(arr0, first.kv)
     first.begin()
+    weight_goes_on(3)
     for d in range(1, full + 1):
         first.advance(d)
+        if d + 3 <= half:
+            weight_goes_on(d + 3)
+        if d + 3 == half:
+            w_all[i, x] = w_ring[pl.ds(x * zs, zs)]
+            for dx in range(1, heads):
+                weight_head(lax.rem(x + dx, heads), x).start()
+    for dx in range(1, heads):
+        weight_head(x, lax.rem(x + dx, heads)).wait_recv()
+    for j in range(1, PLANE):
+        weight_side(j, i).start()
     landed_all(1, arr1)
     unpack(arr1, second.kv)
     second.begin()
@@ -378,127 +476,39 @@
     second.arrive()
     attend(listed, GROUPS[0], GROUPS[1], loc, q_ref, second.kv, second.out, o1)
     give_back(4, o1, back1, ret1)
+    for j in range(1, PLANE):
+        weight_side(j, lax.rem(i + PLANE - j, PLANE)).wait_recv()
+    rows_gathered(0)
+    part = out_ref.shape[1] // 2
+    for p in range(2):
+        total0[:, p * part : (p + 1) * part] = products(rows0, 0, p)
 
     for dz in hops:
         tag(dz, z).wait_send()
     for j in range(1, PLANE):
         tag_side(j, i).wait_send()
+        weight_side(j, i).wait_send()
+    for up in (True, False):
+        for d in range(1, half + 1):
+            if d < half or up:
+                weight_hop(d, up, z).wait_send()
+    for dx in range(1, heads):
+        weight_head(lax.rem(x + dx, heads), x).wait_send()
+        rows_head(0, dx, x).wait_send()
     first.finish()
     second.finish()
-    for n, block in enumerate((send0, send1, sendq, back0, back1)):
+    for n, block in enumerate((send0, send1, sendq, back0)):
         drain(block, total - 1, a2a_send.at[n])
-    receive_back(4, ret1, cut)
-
-
-def project_kernel(planes, rows_ref, weight_ref, order_ref, out_ref, held, sent, came, near, load, send, recv):
-    n = lax.axis_size("head")
-    x = lax.axis_index("head")
-    left, right, opposite = lax.rem(x + n - 1, n), lax.rem(x + 1, n), lax.rem(x + 2, n)
-    width = out_ref.shape[1]
-    part = width // 2
-    piece = width // PLANE
-    owners = (opposite, right, left, x)
-    for at, to in enumerate(owners):
-        for p in range(PLANE):
-            source = pl.multiple_of(p * (n * piece) + to * piece, piece)
-            pltpu.make_async_copy(
-                weight_ref.at[pl.ds(source, piece)], held.at[at, pl.ds(p * piece, piece)], load.at[at]
-            ).start()
-
-    barrier = pltpu.get_barrier_semaphore()
-    for other in (left, right):
-        pl.semaphore_signal(barrier, inc=1, device_id={"head": other}, device_id_type=MESH)
-
-    def block(at, half):
-        return lax.dot_general(
-            rows_ref[...],
-            held[at, half * part : (half + 1) * part],
-            (((1,), (1,)), ((), ())),
-            preferred_element_type=F32,
-        )
-
-    def ready(at):
-        pltpu.make_async_copy(held.at[at], held.at[at], load.at[at]).wait()
-
-    def copy(way, piece, src, dst):
-        return pltpu.make_async_remote_copy(
-            src_ref=src,
-            dst_ref=dst,
-            send_sem=send.at[way, piece],
-            recv_sem=recv.at[way, piece],
-            device_id={"head": right if way == 0 else left},
-            device_id_type=MESH,
-        )
-
-    copies = []
-    for w in range(2):
-        copies.append([copy(w, 0, sent.at[w, 0], near.at[w])])
-        copies[w] += [copy(w, p, sent.at[w, p], came.at[w, p - 1]) for p in (1, 2)]
-    ready(0)
-    for w in range(2):
-        sent[w, 0] = block(0, w).astype(BF16)
-    pl.semaphore_wait(barrier, 2)
-    for w in range(2):
-        copies[w][0].start()
-    for w in range(2):
-        ready(1 + w)
-        sent[w, 1] = block(1 + w, 1 - w).astype(BF16)
-        copies[w][1].start()
-    summed = [block(1 + w, w) for w in range(2)]
-    for w in range(2):
-        copies[w][0].wait_recv()
-        sent[w, 2] = (summed[w].astype(BF16).astype(F32) + near[w].astype(F32)).astype(BF16)
-        copies[w][2].start()
-    ready(3)
-    own = [block(3, h).astype(BF16).astype(F32) for h in range(2)]
-    for w in range(2):
-        copies[w][1].wait_recv()
-    for w in range(2):
-        copies[w][2].wait_recv()
-    result = jnp.zeros(out_ref.shape, F32)
-    for h in range(2):
-        total = own[h]
-        for w in range(2):
-            total = total + came[w, 1 if h == w else 0].astype(F32)
-        result = result + exact(total.astype(BF16), order_ref[h * part : (h + 1) * part])
+    receive_back(4, ret1, 1)
+    drain(back1, total - 1, a2a_send.at[4])
+    rows_gathered(1)
+    result = 0.0
+    for p in range(2):
+        summed = (total0[:, p * part : (p + 1) * part] + products(rows1, cut, p)).astype(BF16)
+        result = result + exact(summed, ordered[p * part : (p + 1) * part])
     out_ref[...] = result.astype(BF16)
-    for w in range(2):
-        for p in range(3):
-            copies[w][p].wait_send()
-
-
-def project(rows, weight, planes):
-    tokens, features = rows.shape
-    heads = lax.axis_size("head")
-    width = weight.shape[0] // heads
-    half = (tokens, width // 2)
-    each = width // PLANE // (planes // heads)
-    order = np.zeros((width, width), np.float32)
-    for p in range(PLANE):
-        for zz in range(planes // heads):
-            for c in range(each):
-                order[(p * (planes // heads) + zz) * each + c, (zz * PLANE + p) * each + c] = 1.0
-    dma = pltpu.SemaphoreType.DMA
-    return pl.pallas_call(
-        functools.partial(project_kernel, planes),
-        out_shape=jax.ShapeDtypeStruct((tokens, width), BF16),
-        in_specs=[VMEM, pl.BlockSpec(memory_space=pl.ANY), VMEM],
-        out_specs=VMEM,
-        scratch_shapes=[
-            pltpu.VMEM((heads, width, features), BF16),
-            pltpu.VMEM((2, 3) + half, BF16),
-            pltpu.VMEM((2, 2) + half, BF16),
-            pltpu.VMEM((2,) + half, BF16),
-            dma((heads,)),
-            dma((2, 3)),
-            dma((2, 3)),
-        ],
-        compiler_params=pltpu.CompilerParams(
-            collective_id=1, has_side_effects=True, vmem_limit_bytes=60 * 2**20
-        ),
-        cost_estimate=pl.CostEstimate(flops=2**31, bytes_accessed=2**23, transcendentals=0),
-        name="project",
-    )(rows, weight, jnp.asarray(order, BF16))
+    for dx in range(1, heads):
+        rows_head(1, dx, x).wait_send()
 
 
 def constants(groups, tokens, quota):
@@ -520,7 +530,18 @@
     return as16(upto), as16(lower), as16(col), as16(col.T), jnp.asarray(col_mask), jnp.asarray(row_mask)
 
 
-def layer(picks, location, labels, slot, query, key, value, groups, quota, listed):
+def column_order(planes, heads, width):
+    zs = planes // heads
+    each = width // PLANE // zs
+    order = np.zeros((width, width), np.float32)
+    for p in range(PLANE):
+        for zz in range(zs):
+            for c in range(each):
+                order[(p * zs + zz) * each + c, (zz * PLANE + p) * each + c] = 1.0
+    return jnp.asarray(order, BF16)
+
+
+def layer(picks, location, labels, slot, query, key, value, weight, groups, heads, quota, listed):
     planes = groups // PLANE
     full = planes // 2 - 2
     tokens, features = query.shape
@@ -532,6 +553,9 @@
         return pltpu.VMEM(shape, BF16)
 
     widths = [heads * HD for heads in GROUPS]
+    each = weight.shape[0]
+    width = each * groups // heads
+    zs = planes // heads
     sends = [scratch(groups, 2 * quota, w) for w in widths + [features // 2]]
     backs = [(groups, 2 * quota, w // 2) for w in widths]
     hots = [scratch(2, slots, tokens), scratch(2, tokens, slots)]
@@ -544,9 +568,9 @@
         rings += [scratch(2, PLANE // 2, *block), scratch(planes * (PLANE - 1), *block)]
         rings += [dma((2, full, SUBS)), dma((2, full, SUBS)), dma((2, 3)), dma((2, 3)), dma, dma]
     return pl.pallas_call(
-        functools.partial(layer_kernel, planes, listed),
-        out_shape=jax.ShapeDtypeStruct((tokens, features), BF16),
-        in_specs=[SMEM, SMEM] + [VMEM] * 12,
+        functools.partial(layer_kernel, planes, heads, listed),
+        out_shape=jax.ShapeDtypeStruct((tokens, width), BF16),
+        in_specs=[SMEM, SMEM] + [VMEM] * 14,
         out_specs=VMEM,
         scratch_shapes=sends
         + [scratch(*b) for b in backs]
@@ -560,10 +584,24 @@
         ]
         + [scratch(*b) for b in backs]
         + [scratch(tokens, w) for w in widths]
+        + [
+            scratch(planes, each, features),
+            scratch(PLANE, heads, zs, each, features),
+        ]
+        + [scratch(heads, tokens, w) for w in widths]
+        + [
+            pltpu.VMEM((tokens, width), F32),
+            dma((2, planes // 2)),
+            dma((2, planes // 2)),
+            dma((2, heads)),
+            dma((2, PLANE)),
+            dma((2, heads)),
+            dma((2, heads)),
+        ]
         + [dma((5,)), dma((5,)), dma((planes,)), dma((planes,)), dma((PLANE,)), dma((PLANE,))]
         + rings,
         compiler_params=pltpu.CompilerParams(
-            collective_id=0, has_side_effects=True, vmem_limit_bytes=56 * 2**20
+            collective_id=0, has_side_effects=True, vmem_limit_bytes=61 * 2**20
         ),
         cost_estimate=pl.CostEstimate(flops=2**32, bytes_accessed=2**27, transcendentals=0),
         name="layer",
@@ -576,7 +614,9 @@
         query,
         key,
         value,
+        weight,
         *constants(groups, tokens, quota),
+        column_order(planes, heads, width),
     )
 
 
@@ -607,7 +647,7 @@
     before = jnp.arange(tokens)[None, :] < jnp.arange(tokens)[:, None]
     rank = jnp.sum((owner[:, None] == owner[None, :]) & before, axis=1, dtype=jnp.int32)
     slot = owner * (2 * quota) + rank
-    token_rows = layer(
+    return layer(
         picks.reshape(-1).astype(jnp.int32),
         location.astype(jnp.int32),
         labels,
@@ -615,13 +655,12 @@
         query,
         key,
         value,
+        out_weight.T,
         groups,
+        lax.axis_size("head"),
         quota,
         listed,
     )
-    weight = lax.all_gather(out_weight.T, "z", axis=0, tiled=True)
-    weight = lax.all_gather(weight, "plane", axis=0, tiled=True)
-    return project(token_rows, weight, planes)
 
 
 def solution(mesh):

time: 414 us -> 403 us (0.973)
  Pallas kernels: 356 us -> 394 us
  blocking collectives: 35.4 us -> 0 us
  between operations: 13.5 us -> 0.1 us
    pallas_call x2 -> x1, Pallas kernels: 356 us -> 394 us  [layer(): pl.pallas_call(functools.partial(layer_kernel, planes, heads, listed), ou...]
    all_gather x1 -> x0, blocking collectives: 35.4 us -> none  [shards(): weight = lax.all_gather(out_weight.T, 'z', axis=0, tiled=True)]
  transfers between devices with their start and end apart: 1 -> 0, of which waited for: 0 -> 0; matrix products, arithmetic and copies ran while one was open for 2% -> 0% of each run, Pallas kernels for 80% -> 0%
where the time goes in v5:
time: 403 us
  Pallas kernels  394 us (98%)
  local copies, waits for them, and re-layouts  6.82 us (2%)
    pallas_call x1, Pallas kernels, layer(): pl.pallas_call(functools.partial(layer_kernel, planes, heads, listed), ou...  394 us

profile of v5, /device:TPU:1, one launch (start us, length us, event | category | flops | bytes accessed | tf_op | source)
XLA Modules:
  0.0 402.8 jit_solution(14350005195581325270)
XLA Ops:
  0.0 0.0 copy-start.1
  0.0 0.0 copy-start.2
  0.0 1.2 copy.19
  1.2 0.0 copy-start
  1.3 0.4 reshape.115
  1.7 0.0 copy-done.1
  1.7 0.0 copy-done.2
  1.7 0.1 compare_select_fusion
  1.8 0.1 reshape.120
  1.9 0.7 gather_fusion
  2.6 0.1 fusion.5
  2.7 0.5 select_reduce_fusion
  3.2 0.7 reshape.116.refs_0_
  3.8 0.5 fusion.7.refs_1_
  4.4 0.0 copy-done
  4.4 0.6 reshape.117.refs_2_
  5.0 0.2 convert_reduce_fusion
  5.2 0.6 convert_element_type.13.refs_3_
  5.8 0.8 convert_element_type.15.refs_4_
  6.5 394.4 %layer.1 = bf16[320,768]{1,0:T(8,128)(2,1)} custom-call(s32[160]{0:T(256)} %reshape.116.refs_0_, s32[60]{0:T(128)} %fusion.7.refs_1_, s32[1,320]{1,0:T(1,128)} %reshape.117.refs_2_, f32[1,320]{1,0:T(1,128)} %convert_element_type.13.refs_3_, f32[320,1]{1,0:T(8,128)} %convert_element_type.15.refs_4_, bf16[320,768]{1,0:T(8,128)(2,1)} %refs_5_.1, ...), custom_call_target="tpu_custom_call" | custom-call | flops 4294967296 | bytes 134217728 | tf_op jit(solution)/shard_map/layer/pallas_call | solution.py:570
  401.0 1.8 copy.22
  (6 shorter events, 0.1 us)
Async XLA Ops:
  0.0 1.7 copy-start.1
  0.0 1.7 copy-start.2
  1.2 3.1 copy-start

commit v6 on v5

--- a/solution.py
+++ b/solution.py
@@ -188,7 +188,7 @@
     (pick, loc, labels_ref, slot_row, slot_col, query, key, value, weight, *rest) = refs
     (upto, lower, col, row, col_mask, row_mask, ordered, out_ref, *rest) = rest
     (send0, send1, sendq, ret0, ret1, packc, packr, arr0, arr1, arrq, all_ref, lab, dcol, drow, q_ref, back0, back1, o0, o1, *rest) = rest
-    (w_ring, w_all, rows0, rows1, total0, w_send, w_recv, w_head, w_side, t_send, t_recv, *rest) = rest
+    (w_ring, w_all, rows0, rows1, total0, w_send, w_recv, w_head, w_chip_send, w_chip_recv, w_core_send, w_core_recv, t_send, t_recv, *rest) = rest
     (a2a_send, a2a_recv, tag_send, tag_recv, tag_side_send, tag_side_recv, *rest) = rest
     per_ring = len(rest) // 2
     z, i = lax.axis_index("z"), lax.axis_index("plane")
@@ -258,7 +258,7 @@
             device_id_type=MESH,
         )
 
-    def exchange(n, block, landed):
+    def exchange(n, block, landed, between=None):
         def start(to):
             pltpu.make_async_remote_copy(
                 src_ref=block.at[to[0] * PLANE + to[1]],
@@ -278,7 +278,12 @@
             start(at(0, j))
             return carry
 
-        lax.fori_loop(0, PLANE, far, 0)
+        if between is None:
+            lax.fori_loop(0, PLANE, far, 0)
+        else:
+            lax.fori_loop(0, PLANE // 2, far, 0)
+            between()
+            lax.fori_loop(PLANE // 2, PLANE, far, 0)
         lax.fori_loop(1, PLANE, close, 0)
         landed[me] = block[me]
 
@@ -323,15 +328,43 @@
             device_id_type=MESH,
         )
 
-    def weight_side(j, source):
-        return pltpu.make_async_remote_copy(
-            src_ref=w_all.at[i],
-            dst_ref=w_all.at[source],
-            send_sem=w_side.at[0, j],
-            recv_sem=w_side.at[1, source],
-            device_id={"plane": lax.rem(i + j, PLANE)},
-            device_id_type=MESH,
-        )
+    chips = PLANE // 2
+    sibling = i + 1 - 2 * (i % 2)
+
+    def of_set(c):
+        return lax.rem(x + c, heads)
+
+    def weight_chip(c, m, source):
+        return pltpu.make_async_remote_copy(
+            src_ref=w_all.at[i, of_set(c)],
+            dst_ref=w_all.at[source, of_set(c)],
+            send_sem=w_chip_send.at[c, m],
+            recv_sem=w_chip_recv.at[c, m],
+            device_id={"plane": lax.rem(i + 2 * m, PLANE)},
+            device_id_type=MESH,
+        )
+
+    def weight_core(c, m, first):
+        at = lax.rem(first + 2 * m, PLANE)
+        return pltpu.make_async_remote_copy(
+            src_ref=w_all.at[at, of_set(c)],
+            dst_ref=w_all.at[at, of_set(c)],
+            send_sem=w_core_send.at[c, m],
+            recv_sem=w_core_recv.at[c, m],
+            device_id={"plane": sibling},
+            device_id_type=MESH,
+        )
+
+    def weight_to_chips(c):
+        for m in range(1, chips):
+            weight_chip(c, m, i).start()
+        weight_core(c, 0, i).start()
+
+    def weight_to_core(c):
+        for m in range(1, chips):
+            weight_chip(c, m, lax.rem(i + PLANE - 2 * m, PLANE)).wait_recv()
+        for m in range(1, chips):
+            weight_core(c, m, i).start()
 
     def rows_head(g, dx, source):
         rows = (rows0, rows1)[g]
@@ -360,17 +393,17 @@
         tag(dz, z).start()
     all_ref[i, z] = labels_ref[...]
     weight_begins()
-    exchange(0, send0, arr0)
+    exchange(0, send0, arr0, lambda: weight_goes_on(1))
     for dz in hops:
         tag(dz, lax.rem(z - dz + planes, planes)).wait_recv()
     for j in range(1, PLANE):
         tag_side(j, i).start()
     to_blocks(packc, columns(key, cut), columns(value, cut), send1)
-    weight_goes_on(1)
+    weight_goes_on(2)
     exchange(1, send1, arr1)
     to_blocks(packc, columns(query, 0), columns(query, query.shape[1] // 2), sendq)
-    weight_goes_on(2)
-    exchange(2, sendq, arrq)
+    weight_goes_on(3)
+    exchange(2, sendq, arrq, lambda: weight_goes_on(4))
     for p in range(2):
         number = lax.broadcasted_iota(jnp.int32, (tokens, slots), 1).astype(F32)
         packr[p] = jnp.where(number == slot_col[...] + float(p * quota), 1.0, 0.0).astype(BF16)
@@ -445,19 +478,20 @@
     landed_all(0, arr0)
     unpack(arr0, first.kv)
     first.begin()
-    weight_goes_on(3)
+    weight_goes_on(5)
     for d in range(1, full + 1):
         first.advance(d)
-        if d + 3 <= half:
-            weight_goes_on(d + 3)
-        if d + 3 == half:
+        if d + 5 <= half:
+            weight_goes_on(d + 5)
+        if d + 5 == half:
             w_all[i, x] = w_ring[pl.ds(x * zs, zs)]
             for dx in range(1, heads):
                 weight_head(lax.rem(x + dx, heads), x).start()
-    for dx in range(1, heads):
-        weight_head(x, lax.rem(x + dx, heads)).wait_recv()
-    for j in range(1, PLANE):
-        weight_side(j, i).start()
+            weight_to_chips(0)
+        if d + 5 > half:
+            c = d + 5 - half
+            weight_head(x, of_set(c)).wait_recv()
+            weight_to_chips(c)
     landed_all(1, arr1)
     unpack(arr1, second.kv)
     second.begin()
@@ -465,19 +499,24 @@
     landed_all(2, arrq)
     unpack(arrq, q_ref)
     second.advance(1)
+    weight_to_core(0)
+    weight_to_core(1)
     first.arrive()
     attend(listed, 0, GROUPS[0], loc, q_ref, first.kv, first.out, o0)
     second.advance(2)
     give_back(3, o0, back0, ret0)
     for d in range(3, full + 1):
         second.advance(d)
+        if d - 1 < heads:
+            weight_to_core(d - 1)
     second.last_hops()
     receive_back(3, ret0, 0)
     second.arrive()
     attend(listed, GROUPS[0], GROUPS[1], loc, q_ref, second.kv, second.out, o1)
     give_back(4, o1, back1, ret1)
-    for j in range(1, PLANE):
-        weight_side(j, lax.rem(i + PLANE - j, PLANE)).wait_recv()
+    for c in range(heads):
+        for m in range(chips):
+            weight_core(c, m, sibling).wait_recv()
     rows_gathered(0)
     part = out_ref.shape[1] // 2
     for p in range(2):
@@ -487,11 +526,15 @@
         tag(dz, z).wait_send()
     for j in range(1, PLANE):
         tag_side(j, i).wait_send()
-        weight_side(j, i).wait_send()
     for up in (True, False):
         for d in range(1, half + 1):
             if d < half or up:
                 weight_hop(d, up, z).wait_send()
+    for c in range(heads):
+        for m in range(chips):
+            if m:
+                weight_chip(c, m, i).wait_send()
+            weight_core(c, m, i).wait_send()
     for dx in range(1, heads):
         weight_head(lax.rem(x + dx, heads), x).wait_send()
         rows_head(0, dx, x).wait_send()
@@ -594,7 +637,7 @@
             dma((2, planes // 2)),
             dma((2, planes // 2)),
             dma((2, heads)),
-            dma((2, PLANE)),
+            *[dma((heads, PLANE // 2))] * 4,
             dma((2, heads)),
             dma((2, heads)),
         ]

time: 403 us -> 359 us (0.89)
  Pallas kernels: 394 us -> 351 us
    pallas_call x1, Pallas kernels: 394 us -> 351 us  [layer(): pl.pallas_call(functools.partial(layer_kernel, planes, heads, listed), ou...]
where the time goes in v6:
time: 359 us
  Pallas kernels  351 us (98%)
  local copies, waits for them, and re-layouts  6.82 us (2%)
    pallas_call x1, Pallas kernels, layer(): pl.pallas_call(functools.partial(layer_kernel, planes, heads, listed), ou...  351 us

profile of v6, /device:TPU:1, one launch (start us, length us, event | category | flops | bytes accessed | tf_op | source)
XLA Modules:
  0.0 359.1 jit_solution(17672763634650335738)
XLA Ops:
  0.0 0.0 copy-start.1
  0.0 0.0 copy-start.2
  0.0 1.2 copy.19
  1.2 0.0 copy-start
  1.3 0.4 reshape.115
  1.7 0.0 copy-done.1
  1.7 0.0 copy-done.2
  1.7 0.1 compare_select_fusion
  1.8 0.1 reshape.120
  1.9 0.7 gather_fusion
  2.6 0.1 fusion.5
  2.7 0.5 select_reduce_fusion
  3.2 0.7 reshape.116.refs_0_
  3.8 0.5 fusion.7.refs_1_
  4.4 0.0 copy-done
  4.4 0.6 reshape.117.refs_2_
  5.0 0.2 convert_reduce_fusion
  5.2 0.6 convert_element_type.13.refs_3_
  5.8 0.8 convert_element_type.15.refs_4_
  6.5 350.7 %layer.1 = bf16[320,768]{1,0:T(8,128)(2,1)} custom-call(s32[160]{0:T(256)} %reshape.116.refs_0_, s32[60]{0:T(128)} %fusion.7.refs_1_, s32[1,320]{1,0:T(1,128)} %reshape.117.refs_2_, f32[1,320]{1,0:T(1,128)} %convert_element_type.13.refs_3_, f32[320,1]{1,0:T(8,128)} %convert_element_type.15.refs_4_, bf16[320,768]{1,0:T(8,128)(2,1)} %refs_5_.1, ...), custom_call_target="tpu_custom_call" | custom-call | flops 4294967296 | bytes 134217728 | tf_op jit(solution)/shard_map/layer/pallas_call | solution.py:613
  357.3 1.8 copy.22
  (6 shorter events, 0.1 us)
Async XLA Ops:
  0.0 1.7 copy-start.1
  0.0 1.7 copy-start.2
  1.2 3.1 copy-start

commit v7 on v6

--- a/solution.py
+++ b/solution.py
@@ -85,12 +85,14 @@
             device_id_type=MESH,
         )
 
-    def spread(self, k, held):
-        self.out[k * PLANE + self.i] = held[self.pick[k * PLANE]]
-        for j in range(1, PLANE):
-            at = k * (PLANE - 1) + j - 1
-            self.stage[at] = held[self.pick[k * PLANE + j]]
-            self.side(k, j, self.stage.at[at]).start()
+    def spread(self, k, held, these):
+        for j in these:
+            if j == 0:
+                self.out[k * PLANE + self.i] = held[self.pick[k * PLANE]]
+            else:
+                at = k * (PLANE - 1) + j - 1
+                self.stage[at] = held[self.pick[k * PLANE + j]]
+                self.side(k, j, self.stage.at[at]).start()
 
     def pass_out(self, k, j, src):
         if j == 0:
@@ -102,7 +104,7 @@
         for s in range(SUBS):
             for up in (True, False):
                 self.hop(1, s, up).start()
-        self.spread(0, self.kv)
+        self.waiting = [(0, self.kv)]
 
     def advance(self, d):
         for s in range(SUBS):
@@ -110,6 +112,10 @@
                 self.hop(d, s, up).wait_recv()
                 if d < self.full:
                     self.hop(d + 1, s, up).start()
+            each = PLANE // SUBS
+            for k, held in self.waiting:
+                self.spread(k, held, range(s * each, (s + 1) * each))
+        self.waiting = [(d, self.ups[d]), (self.planes - d, self.downs[d])]
         if d == self.full:
             for up in (True, False):
                 n = 0 if up else 1
@@ -121,8 +127,8 @@
                 for j in range(PLANE):
                     self.packs[n, self.part + j] = held[self.pick[base + PLANE + j]]
                 self.pack(1, up).start()
-        self.spread(d, self.ups[d])
-        self.spread(self.planes - d, self.downs[d])
+            for k, held in self.waiting:
+                self.spread(k, held, range(PLANE))
 
     def last_hops(self):
         for up in (True, False):
@@ -258,7 +264,7 @@
             device_id_type=MESH,
         )
 
-    def exchange(n, block, landed, between=None):
+    def exchange(n, block, landed, between=None, halves=(0, 1)):
         def start(to):
             pltpu.make_async_remote_copy(
                 src_ref=block.at[to[0] * PLANE + to[1]],
@@ -278,14 +284,14 @@
             start(at(0, j))
             return carry
 
-        if between is None:
-            lax.fori_loop(0, PLANE, far, 0)
-        else:
+        if 0 in halves:
             lax.fori_loop(0, PLANE // 2, far, 0)
+        if between is not None:
             between()
+        if 1 in halves:
             lax.fori_loop(PLANE // 2, PLANE, far, 0)
-        lax.fori_loop(1, PLANE, close, 0)
-        landed[me] = block[me]
+            lax.fori_loop(1, PLANE, close, 0)
+            landed[me] = block[me]
 
     def landed_all(n, landed):
         drain(landed, total - 1, a2a_recv.at[n])
@@ -455,9 +461,9 @@
 
         from_blocks(drow, landed, store)
 
-    def give_back(n, attended, back, ret):
+    def give_back(n, attended, back, ret, halves=(0, 1)):
         to_blocks(dcol, columns(attended, 0), columns(attended, back.shape[2]), back)
-        exchange(n, back, ret)
+        exchange(n, back, ret, None, halves)
 
     def receive_back(n, ret, g):
         rows = (rows0, rows1)[g]
@@ -504,16 +510,17 @@
     first.arrive()
     attend(listed, 0, GROUPS[0], loc, q_ref, first.kv, first.out, o0)
     second.advance(2)
-    give_back(3, o0, back0, ret0)
+    give_back(3, o0, back0, ret0, (0,))
     for d in range(3, full + 1):
         second.advance(d)
         if d - 1 < heads:
             weight_to_core(d - 1)
     second.last_hops()
-    receive_back(3, ret0, 0)
+    exchange(3, back0, ret0, None, (1,))
     second.arrive()
     attend(listed, GROUPS[0], GROUPS[1], loc, q_ref, second.kv, second.out, o1)
     give_back(4, o1, back1, ret1)
+    receive_back(3, ret0, 0)
     for c in range(heads):
         for m in range(chips):
             weight_core(c, m, sibling).wait_recv()

time: 359 us -> 354 us (0.986)
  Pallas kernels: 351 us -> 345 us
    pallas_call x1, Pallas kernels: 351 us -> 345 us  [layer(): pl.pallas_call(functools.partial(layer_kernel, planes, heads, listed), ou...]
where the time goes in v7:
time: 354 us
  Pallas kernels  345 us (97%)
  local copies, waits for them, and re-layouts  6.82 us (2%)
    pallas_call x1, Pallas kernels, layer(): pl.pallas_call(functools.partial(layer_kernel, planes, heads, listed), ou...  345 us

profile of v7, /device:TPU:1, one launch (start us, length us, event | category | flops | bytes accessed | tf_op | source)
XLA Modules:
  0.0 353.9 jit_solution(1678086246789460013)
XLA Ops:
  0.0 0.0 copy-start.1
  0.0 0.0 copy-start.2
  0.0 1.2 copy.19
  1.2 0.0 copy-start
  1.3 0.4 reshape.115
  1.7 0.0 copy-done.1
  1.7 0.0 copy-done.2
  1.7 0.1 compare_select_fusion
  1.8 0.1 reshape.120
  1.9 0.7 gather_fusion
  2.6 0.1 fusion.5
  2.7 0.5 select_reduce_fusion
  3.2 0.7 reshape.116.refs_0_
  3.8 0.5 fusion.7.refs_1_
  4.4 0.0 copy-done
  4.4 0.6 reshape.117.refs_2_
  5.0 0.2 convert_reduce_fusion
  5.2 0.6 convert_element_type.13.refs_3_
  5.8 0.8 convert_element_type.15.refs_4_
  6.5 345.5 %layer.1 = bf16[320,768]{1,0:T(8,128)(2,1)} custom-call(s32[160]{0:T(256)} %reshape.116.refs_0_, s32[60]{0:T(128)} %fusion.7.refs_1_, s32[1,320]{1,0:T(1,128)} %reshape.117.refs_2_, f32[1,320]{1,0:T(1,128)} %convert_element_type.13.refs_3_, f32[320,1]{1,0:T(8,128)} %convert_element_type.15.refs_4_, bf16[320,768]{1,0:T(8,128)(2,1)} %refs_5_.1, ...), custom_call_target="tpu_custom_call" | custom-call | flops 4294967296 | bytes 134217728 | tf_op jit(solution)/shard_map/layer/pallas_call | solution.py:620
  352.0 1.8 copy.22
  (6 shorter events, 0.1 us)
Async XLA Ops:
  0.0 1.7 copy-start.1
  0.0 1.7 copy-start.2
  1.2 3.1 copy-start

commit v8 on v7

--- a/solution.py
+++ b/solution.py
@@ -521,13 +521,7 @@
     attend(listed, GROUPS[0], GROUPS[1], loc, q_ref, second.kv, second.out, o1)
     give_back(4, o1, back1, ret1)
     receive_back(3, ret0, 0)
-    for c in range(heads):
-        for m in range(chips):
-            weight_core(c, m, sibling).wait_recv()
-    rows_gathered(0)
-    part = out_ref.shape[1] // 2
-    for p in range(2):
-        total0[:, p * part : (p + 1) * part] = products(rows0, 0, p)
+    receive_back(4, ret1, 1)
 
     for dz in hops:
         tag(dz, z).wait_send()
@@ -544,12 +538,17 @@
             weight_core(c, m, i).wait_send()
     for dx in range(1, heads):
         weight_head(lax.rem(x + dx, heads), x).wait_send()
-        rows_head(0, dx, x).wait_send()
     first.finish()
     second.finish()
     for n, block in enumerate((send0, send1, sendq, back0)):
         drain(block, total - 1, a2a_send.at[n])
-    receive_back(4, ret1, 1)
+    for c in range(heads):
+        for m in range(chips):
+            weight_core(c, m, sibling).wait_recv()
+    rows_gathered(0)
+    part = out_ref.shape[1] // 2
+    for p in range(2):
+        total0[:, p * part : (p + 1) * part] = products(rows0, 0, p)
     drain(back1, total - 1, a2a_send.at[4])
     rows_gathered(1)
     result = 0.0
@@ -558,6 +557,7 @@
         result = result + exact(summed, ordered[p * part : (p + 1) * part])
     out_ref[...] = result.astype(BF16)
     for dx in range(1, heads):
+        rows_head(0, dx, x).wait_send()
         rows_head(1, dx, x).wait_send()
 
 

time: 354 us -> 350 us (0.989)
    pallas_call x1, Pallas kernels: 345 us -> 342 us  [layer(): pl.pallas_call(functools.partial(layer_kernel, planes, heads, listed), ou...]
where the time goes in v8:
time: 350 us
  Pallas kernels  342 us (98%)
  local copies, waits for them, and re-layouts  6.82 us (2%)
    pallas_call x1, Pallas kernels, layer(): pl.pallas_call(functools.partial(layer_kernel, planes, heads, listed), ou...  342 us

profile of v8, /device:TPU:1, one launch (start us, length us, event | category | flops | bytes accessed | tf_op | source)
XLA Modules:
  0.0 350.0 jit_solution(6702134325515838699)
XLA Ops:
  0.0 0.0 copy-start.1
  0.0 0.0 copy-start.2
  0.0 1.2 copy.19
  1.2 0.0 copy-start
  1.3 0.4 reshape.115
  1.7 0.0 copy-done.1
  1.7 0.0 copy-done.2
  1.7 0.1 compare_select_fusion
  1.8 0.1 reshape.120
  1.9 0.7 gather_fusion
  2.6 0.1 fusion.5
  2.7 0.5 select_reduce_fusion
  3.2 0.7 reshape.116.refs_0_
  3.8 0.5 fusion.7.refs_1_
  4.4 0.0 copy-done
  4.4 0.6 reshape.117.refs_2_
  5.0 0.2 convert_reduce_fusion
  5.2 0.6 convert_element_type.13.refs_3_
  5.8 0.8 convert_element_type.15.refs_4_
  6.5 341.6 %layer.1 = bf16[320,768]{1,0:T(8,128)(2,1)} custom-call(s32[160]{0:T(256)} %reshape.116.refs_0_, s32[60]{0:T(128)} %fusion.7.refs_1_, s32[1,320]{1,0:T(1,128)} %reshape.117.refs_2_, f32[1,320]{1,0:T(1,128)} %convert_element_type.13.refs_3_, f32[320,1]{1,0:T(8,128)} %convert_element_type.15.refs_4_, bf16[320,768]{1,0:T(8,128)(2,1)} %refs_5_.1, ...), custom_call_target="tpu_custom_call" | custom-call | flops 4294967296 | bytes 134217728 | tf_op jit(solution)/shard_map/layer/pallas_call | solution.py:620
  348.2 1.8 copy.22
  (6 shorter events, 0.1 us)
Async XLA Ops:
  0.0 1.7 copy-start.1
  0.0 1.7 copy-start.2
  1.2 3.1 copy-start
